TPU v7x, 128 devices: a whole 4x4x4 slice. The times are simulated.
128 devices in a mesh: batch: 4 (over z_lo, core), seq: 32 (over y, x, z_hi).
Axes of the slice: x: 4, y: 4, z: 4 (z_hi: 2, z_lo: 2; z = z_hi * 2 + z_lo), core: 2. Of those that a mesh axis runs over, the one named last changes fastest.
Arguments:
- tokens: bfloat16 [4, 4096, 512], P('batch', 'seq'), may hold values from -6 to 6
- camera: bfloat16 [4, 1024], P('batch'), may hold values from -6 to 6
- features: bfloat16 [4, 1024, 384], P('batch', 'seq'), may hold values from -6 to 6
- foreground: int32 [4, 8], P('batch'), may hold values from 0 to 1, as said below
- layout: int32 [4, 32], P('batch', 'seq'), may hold values from 0 to 31, as said below
- modulation_weight: bfloat16 [1024, 1024], replicated, may hold values from -0.09375 to 0.09375
- modulation_bias: bfloat16 [1024], replicated, may hold values from -3 to 3
- self_in_weight: bfloat16 [512, 1536], replicated, may hold values from -0.25 to 0.25
- self_out_weight: bfloat16 [512, 512], replicated, may hold values from -0.75 to 0.75
- cross_norm_gain: bfloat16 [512], replicated, may hold values from 0.25 to 1.75
- cross_norm_bias: bfloat16 [512], replicated, may hold values from -2 to 2
- cross_query_weight: bfloat16 [512, 512], replicated, may hold values from -0.375 to 0.375
- cross_pair_weight: bfloat16 [384, 1024], replicated, may hold values from -0.4375 to 0.4375
- cross_out_weight: bfloat16 [512, 512], replicated, may hold values from -0.75 to 0.75
- feed_norm_gain: bfloat16 [512], replicated, may hold values from 0.25 to 1.75
- feed_norm_bias: bfloat16 [512], replicated, may hold values from -2 to 2
- up_weight: bfloat16 [512, 2048], replicated, may hold values from -0.25 to 0.25
- down_weight: bfloat16 [2048, 512], replicated, may hold values from -0.125 to 0.125
- cotangent: bfloat16 [4, 4096, 512], P('batch', 'seq'), may hold values from -6 to 6
Outputs:
- block_out: float32 [4, 4096, 512], P('batch', 'seq')
- token_grad: float32 [4, 4096, 512], P('batch', 'seq')
- feature_grad: float32 [4, 1024, 384], P('batch', 'seq')
- modulation_weight_grad: float32 [1024, 1024], replicated
- modulation_bias_grad: float32 [1024], replicated
- self_in_weight_grad: float32 [512, 1536], replicated
- self_out_weight_grad: float32 [512, 512], replicated
- cross_norm_gain_grad: float32 [512], replicated
- cross_norm_bias_grad: float32 [512], replicated
- cross_query_weight_grad: float32 [512, 512], replicated
- cross_pair_weight_grad: float32 [384, 1024], replicated
- cross_out_weight_grad: float32 [512, 512], replicated
- feed_norm_gain_grad: float32 [512], replicated
- feed_norm_bias_grad: float32 [512], replicated
- up_weight_grad: float32 [512, 2048], replicated
- down_weight_grad: float32 [2048, 512], replicated
Inputs may be any that keep to these rules, and one draw needn't show every extreme that they name: Each object has at least one patch block with foreground and at least one without. `layout`: each row is a permutation of 0 to 31. Block numbers below 24 are triplane blocks; block number b of 24 or more is patch block b - 24.
All inputs are finite; a program needn't handle non-finite values.
Results may differ from a plain program's by a relative error of at most 0.04.
Values may be sent and summed in bfloat16 or wider, within the bound.
No kernel may reach another device: no remote copies, remote signals or barrier semaphores. Data moves between devices by JAX's collectives and lax.ppermute only.
A program may use at most 192 MiB of HBM per device.

v0:
```python
import functools

import jax
import jax.numpy as jnp
from jax import lax
from jax.experimental import pallas as pl
from jax.experimental.pallas import tpu as pltpu
from jax.sharding import PartitionSpec as P

HEADS = 8
HEAD_DIM = 64
BLOCK = 128
TRIB = 24
PATCHB = 8
WIDTH = 512
PATCHES = 1024
TOKENS = 4096
EPSILON = 1e-05
MASKED = -1e30
FLAG = 3e38
SCALE = HEAD_DIM ** (-0.5)
BF = jnp.bfloat16
F32 = jnp.float32
AXES = ("batch", "seq")
PEERS = 32
QUARTERS = 4
SHARE = BLOCK // QUARTERS
MIB = 1024 * 1024


def nn(a, b):
    return lax.dot_general(a, b, (((1,), (0,)), ((), ())), preferred_element_type=F32)


def nt(a, b):
    return lax.dot_general(a, b, (((1,), (1,)), ((), ())), preferred_element_type=F32)


def tn(a, b):
    return lax.dot_general(a, b, (((0,), (0,)), ((), ())), preferred_element_type=F32)


def half_turn(values):
    return pltpu.roll(values, 64, 1)


def low_lanes(rows):
    return lax.broadcasted_iota(jnp.int32, (rows, 128), 1) < 64


def norm_parts(values):
    centre = jnp.mean(values, axis=-1, keepdims=True)
    centred = values - centre
    spread = jnp.mean(centred * centred, axis=-1, keepdims=True)
    inverse = lax.rsqrt(spread + EPSILON)
    return centred * inverse, inverse


def norm_back(normed, inverse, grad):
    first = jnp.mean(grad, axis=-1, keepdims=True)
    second = jnp.mean(grad * normed, axis=-1, keepdims=True)
    return inverse * (grad - first - normed * second)


class Late:
    def __init__(self, copy, ref):
        self.copy, self.ref, self.here, self.shape = copy, ref, False, ref.shape

    def ready(self):
        if not self.here:
            self.copy.wait()
            self.here = True
        return self.ref

    def __getitem__(self, index):
        return self.ready()[index]


class Away:
    def __init__(self, ref, copy):
        self.ref, self.copy, self.sent, self.shape = ref, copy, False, ref.shape

    def __setitem__(self, index, value):
        self.ref[index] = value

    def send(self):
        if not self.sent:
            self.copy.start()
            self.sent = True


def call(
    kernel, out_shape, inputs, scratch=(), flops=0, traffic=0, limit=32, smem=(), late=(), away=(), far_out=(),
    far_in=(), aliases=None,
):
    vmem = pl.BlockSpec(memory_space=pltpu.VMEM)
    scalar = pl.BlockSpec(memory_space=pltpu.SMEM)
    far = pl.BlockSpec(memory_space=pltpu.HBM)
    single = not isinstance(out_shape, tuple)
    outs = (out_shape,) if single else out_shape
    count, extra = len(inputs), len(scratch)
    def whole(*refs):
        refs = list(refs)
        ins, results = refs[:count], refs[count : count + len(outs)]
        rest = refs[count + len(outs) :]
        mine, buffers = rest[:extra], rest[extra:]
        semaphores = buffers[-1] if late or away else None
        for k, which in enumerate(late):
            copy = pltpu.make_async_copy(ins[which], buffers[k], semaphores.at[k])
            copy.start()
            ins[which] = Late(copy, buffers[k])
        for k, which in enumerate(away):
            buffer = buffers[len(late) + k]
            results[which] = Away(
                buffer, pltpu.make_async_copy(buffer, results[which], semaphores.at[len(late) + k])
            )
        kernel(*ins, *results, *mine)
        for which in late:
            ins[which].ready()
        for which in away:
            results[which].send()
        for which in away:
            results[which].copy.wait()

    buffers = [pltpu.VMEM(inputs[k].shape, inputs[k].dtype) for k in late]
    buffers += [pltpu.VMEM(outs[k].shape, outs[k].dtype) for k in away]
    if buffers:
        buffers.append(pltpu.SemaphoreType.DMA((len(buffers),)))
    out_specs = tuple(far if k in away or k in far_out else vmem for k in range(len(outs)))
    return pl.pallas_call(
        whole,
        out_shape=out_shape,
        in_specs=[scalar if k in smem else far if k in late or k in far_in else vmem for k in range(count)],
        out_specs=out_specs[0] if single else out_specs,
        scratch_shapes=list(scratch) + buffers,
        input_output_aliases=aliases or {},
        compiler_params=pltpu.CompilerParams(vmem_limit_bytes=limit * MIB),
        cost_estimate=pl.CostEstimate(
            flops=int(flops), bytes_accessed=int(traffic), transcendentals=0
        ),
    )(*inputs)


def shape(dims, dtype=F32):
    return jax.ShapeDtypeStruct(dims, dtype)


def prepare_kernel(
    foreground, layout, tokens, features, camera, mod_weight, mod_bias, in_weight,
    far_message, modulation, message, semaphores,
):
    for to in range(PEERS):
        for k in range(3):
            message[to, 144 + 32 * k : 176 + 32 * k, :] = features[:, 128 * k : 128 * (k + 1)]
    cam = camera[...].astype(F32)
    cam_act = (cam * jax.nn.sigmoid(cam)).astype(BF)
    mod = nn(jnp.broadcast_to(cam_act, (16, cam_act.shape[1])), mod_weight[...])[0:8]
    mod = mod + mod_bias[...].astype(F32).reshape(1, 2 * WIDTH)
    modulation[...] = mod
    block = layout[0, 0]
    lit = jnp.int32(0)
    for k in range(PATCHB):
        lit = lit + jnp.where(block - TRIB == k, foreground[0, k], 0)
    kept = jnp.logical_or(block < TRIB, lit > 0)
    normed, _ = norm_parts(tokens[...].astype(F32))
    hidden = (normed * (1.0 + mod[0:1, :WIDTH]) + mod[0:1, WIDTH:]).astype(BF)
    projected = nn(hidden, in_weight[...]).astype(BF).astype(F32)
    low = low_lanes(BLOCK)
    low_half = low_lanes(16)
    corner = jnp.logical_and(
        lax.broadcasted_iota(jnp.int32, (BLOCK, 128), 0) == 0, lax.broadcasted_iota(jnp.int32, (BLOCK, 128), 1) == 0
    )
    flagged = jnp.logical_and(corner, jnp.logical_not(kept))
    for pair in range(HEADS // 2):
        at = 128 * pair
        query = projected[:, at : at + 128] * SCALE
        key = projected[:, WIDTH + at : WIDTH + at + 128]
        value = projected[:, 2 * WIDTH + at : 2 * WIDTH + at + 128]
        query_turned = half_turn(query)
        for odd in range(2):
            head = 2 * pair + odd
            if odd:
                both = jnp.where(low, half_turn(key), value)
                first, second = query_turned, query
            else:
                both = jnp.where(low, key, half_turn(value))
                first, second = query, query_turned
            both = jnp.where(flagged, FLAG, both).astype(BF)
            for quarter in range(QUARTERS):
                to = QUARTERS * head + quarter
                message[to, 0:128, :] = both
                top = SHARE * quarter
                message[to, 128:144, :] = jnp.where(
                    low_half, first[top : top + 16], second[top + 16 : top + 32]
                ).astype(BF)
            some = slice(QUARTERS * head, QUARTERS * (head + 1))
            pltpu.make_async_copy(message.at[some], far_message.at[some], semaphores.at[head]).start()
    for head in range(HEADS):
        some = slice(QUARTERS * head, QUARTERS * (head + 1))
        pltpu.make_async_copy(message.at[some], far_message.at[some], semaphores.at[head]).wait()


def loop(count, work, unroll=1):
    def turn(k, carry):
        work(k)
        return carry

    lax.fori_loop(0, count, turn, 0, unroll=unroll)


def block_of(k, size):
    return pl.ds(pl.multiple_of(k * size, size), size)


def gather_keys(received, masked_keys, pairs, queries, turned):
    low = low_lanes(128)
    lane = lax.broadcasted_iota(jnp.int32, (128, 128), 1)
    lane_q = lax.broadcasted_iota(jnp.int32, (16, 128), 1)
    extra = jnp.where(lane_q == 64, 1.0, 0.0)

    def gather(k):
        at = block_of(k, 128)
        both = received[k, 0:128, :].astype(F32)
        mine = received[k, 128:144, :].astype(F32)
        masked = both[0:1, 0:1] > 1e38
        masked_keys[at, :] = jnp.where(
            low, jnp.where(masked, 0.0, both), jnp.where(jnp.logical_and(masked, lane == 64), MASKED, 0.0)
        ).astype(BF)
        if pairs is not None:
            pairs[at, :] = received[k, 0:128, :]
        if turned is not None:
            turned[:, at] = jnp.transpose(both).astype(BF)
        first = pl.ds(pl.multiple_of(SHARE * k, 16), 16)
        second = pl.ds(pl.multiple_of(SHARE * k + 16, 16), 16)
        queries[first, :] = jnp.where(lane_q < 64, mine, extra).astype(BF)
        queries[second, :] = jnp.where(lane_q < 64, half_turn(mine), extra).astype(BF)

    loop(PEERS, gather, 4)


KEYS = 512
ROWS = 1024
UNROLL_A = 2
UNROLL_B = 4
UNROLL_C = 1
BACK_KEYS = 1024
BACK_ROWS = 256
QUERIES = PEERS * SHARE


def attend_kernel(
    received, message, attended, log_total, pairs_turned, masked_keys, queries, scores, mixed, turned
):
    gather_keys(received, masked_keys, None, queries, pairs_turned)
    chunks = TOKENS // KEYS
    query = queries[...]

    def score(k, top):
        at = block_of(k, KEYS)
        part = nt(masked_keys[at, :], query)
        scores[at, :] = part
        return jnp.maximum(top, jnp.max(part, axis=0, keepdims=True))

    top = lax.fori_loop(0, chunks, score, jnp.full((1, ROWS), -jnp.inf, F32), unroll=UNROLL_A)
    mixed[...] = jnp.zeros_like(mixed)

    def mix(k, total):
        at = block_of(k, KEYS)
        chance = jnp.exp(scores[at, :] - top)
        mixed[...] += nn(pairs_turned[:, at], chance.astype(BF))
        return total + jnp.sum(chance, axis=0, keepdims=True)

    total = lax.fori_loop(0, chunks, mix, jnp.zeros((1, ROWS), F32), unroll=UNROLL_B)
    result = mixed[...] / total
    attended[...] = result[64:128, :]
    log_total[...] = jnp.broadcast_to(top + jnp.log(total), (8, ROWS))
    turned[...] = jnp.transpose(result)
    low = low_lanes(16)

    def pack(k):
        first = turned[pl.ds(pl.multiple_of(SHARE * k, 16), 16), :]
        second = turned[pl.ds(pl.multiple_of(SHARE * k + 16, 16), 16), :]
        message[k] = jnp.where(low, half_turn(first), second).astype(BF)

    loop(PEERS, pack, 4)


def pairs_kernel(
    received, pair_weight, keys, values, keys_turned, values_turned, every_turned, kept, every
):
    pair_weight = pair_weight.ready()

    def gather(k):
        for j in range(3):
            every[block_of(k, 32), 128 * j : 128 * (j + 1)] = received[k, 144 + 32 * j : 176 + 32 * j, :]
        kept.ref[k] = received[k, 0:144, :]

    def project(k):
        rows = block_of(k, 256)
        part = every[rows, :]
        every_turned.ref[:, rows] = jnp.transpose(part.astype(F32)).astype(BF)
        both = nn(part, pair_weight[...]).astype(BF)
        keys.ref[rows, :] = both[:, :WIDTH]
        values.ref[rows, :] = both[:, WIDTH:]
        turned = jnp.transpose(both.astype(F32)).astype(BF)
        keys_turned.ref[:, rows] = turned[:WIDTH, :]
        values_turned.ref[:, rows] = turned[WIDTH:, :]

    loop(PEERS, gather, 4)
    kept.send()
    loop(PATCHES // 256, project)


def unpack_heads(received):
    low = low_lanes(16)
    columns = []
    for pair in range(HEADS // 2):
        pieces = []
        for quarter in range(QUARTERS):
            even = received[QUARTERS * (2 * pair) + quarter].astype(F32)
            odd = received[QUARTERS * (2 * pair + 1) + quarter].astype(F32)
            pieces.append(jnp.where(low, even, half_turn(odd)))
            pieces.append(jnp.where(low, half_turn(even), odd))
        columns.append(jnp.concatenate(pieces, axis=0))
    return jnp.concatenate(columns, axis=1)


def pack_heads(values, message):
    low = low_lanes(16)
    for pair in range(HEADS // 2):
        for quarter in range(QUARTERS):
            first = values[SHARE * quarter : SHARE * quarter + 16, 128 * pair : 128 * (pair + 1)]
            second = values[SHARE * quarter + 16 : SHARE * (quarter + 1), 128 * pair : 128 * (pair + 1)]
            message[QUARTERS * (2 * pair) + quarter] = jnp.where(
                low, first, half_turn(second)
            ).astype(BF)
            message[QUARTERS * (2 * pair + 1) + quarter] = jnp.where(
                low, half_turn(first), second
            ).astype(BF)


GELU = 0.7978845608028654
CUBE = 0.044715


def put(place, keep, send, owner, rows, value):
    @pl.when(place[0] == owner)
    def _():
        keep[rows, :] = value

    @pl.when(place[0] != owner)
    def _():
        send[rows, :] = value


def middle_kernel(
    place, received, tokens, keys, keys_turned, values, values_turned, self_out, gain_two, offset_two,
    query_weight, cross_out, gain_three, offset_three, up_weight, down_weight, cotangent, every_turned, pair_weight,
    block_out, feed_keep, feed_send, vectors, message, self_grad, feature_part, pair_value,
    feed_pack, semaphores, key_all, value_all, total_out, total_back,
):
    def move(start, rows, to, slot):
        at = slice(to, to + rows)

        @pl.when(place[0] == 0)
        def _():
            pltpu.make_async_copy(feed_pack.at[0, start : start + rows], feed_keep.at[at], semaphores.at[slot, 0]).start()
            pltpu.make_async_copy(feed_pack.at[1, start : start + rows], feed_send.at[at], semaphores.at[slot, 1]).start()

        @pl.when(place[0] != 0)
        def _():
            pltpu.make_async_copy(feed_pack.at[1, start : start + rows], feed_keep.at[at], semaphores.at[slot, 0]).start()
            pltpu.make_async_copy(feed_pack.at[0, start : start + rows], feed_send.at[at], semaphores.at[slot, 1]).start()

    def put_halves(start, value):
        rows = value.shape[0] // 2
        feed_pack[0, start : start + rows, :] = value[:rows]
        feed_pack[1, start : start + rows, :] = value[rows:]

    attended_low = unpack_heads(received).astype(BF)
    first = tokens[...].astype(F32) + nn(attended_low, self_out[...])
    normed_two, inverse_two = norm_parts(first)
    gain = gain_two[...].astype(F32)
    hidden = (normed_two * gain + offset_two[...].astype(F32)).astype(BF)
    queries = nn(hidden, query_weight[...]).astype(BF).astype(F32) * SCALE
    low = low_lanes(BLOCK)
    upper = lax.broadcasted_iota(jnp.int32, (128, BLOCK), 0) < 64
    masked = []
    chances = []
    pieces = []
    for pair in range(HEADS // 2):
        at = slice(128 * pair, 128 * (pair + 1))
        key = keys[:, at]
        value = values_turned[at, :]
        parts = []
        for odd in range(2):
            mine = jnp.where(low if odd == 0 else jnp.logical_not(low), queries[:, at], 0.0).astype(BF)
            scores = nt(key, mine)
            chance = jnp.exp(scores - jnp.max(scores, axis=0, keepdims=True))
            chance = chance * (1.0 / jnp.sum(chance, axis=0, keepdims=True))
            masked.append(mine)
            chances.append(chance)
            parts.append(nn(value, chance.astype(BF)))
        pieces.append(jnp.transpose(jnp.where(upper, parts[0], parts[1])))
    mixed = jnp.concatenate(pieces, axis=1).astype(BF)
    second = first + nn(mixed, cross_out[...])
    normed, inverse = norm_parts(second)
    gain_out = gain_three[...].astype(F32)
    hidden3 = (normed * gain_out + offset_three[...].astype(F32)).astype(BF)
    grad_low = cotangent[...]
    total_out[...] = second
    total_back[...] = jnp.zeros((BLOCK, WIDTH), F32)
    up_all, down_all = up_weight.ready(), down_weight.ready()

    def feed_block(k, carry):
        at = pl.ds(pl.multiple_of(512 * k, 512), 512)
        up, down = up_all[:, at], down_all[at, :]
        pre = nn(hidden3, up)
        square = pre * pre
        turn = jnp.tanh(GELU * (pre + CUBE * (square * pre)))
        half = 0.5 * (1.0 + turn)
        active = (pre * half).astype(BF)
        slope = half + (0.5 * pre) * (1.0 - turn * turn) * (GELU * (1.0 + (3.0 * CUBE) * square))
        total_out[...] += nn(active, down)
        pre_grad = (nt(grad_low, down) * slope).astype(BF)
        total_back[...] += nt(pre_grad, up)
        grad = tn(hidden3, pre_grad).astype(BF)
        feed_pack[0, pl.ds(pl.multiple_of(256 * k, 256), 256), :] = grad[:256]
        feed_pack[1, pl.ds(pl.multiple_of(256 * k, 256), 256), :] = grad[256:]
        feed_pack[k // 2, pl.ds(pl.multiple_of(1024 + 512 * (k % 2), 512), 512), :] = tn(active, grad_low).astype(BF)
        return carry

    lax.fori_loop(0, 4, feed_block, 0, unroll=1)
    result = total_out[...]
    back = total_back[...]
    move(0, 2048, 0, 0)
    block_out[...] = result
    vectors[2:3, :] = jnp.sum(back * normed, axis=0, keepdims=True)
    vectors[3:4, :] = jnp.sum(back, axis=0, keepdims=True)
    grad = grad_low.astype(F32) + norm_back(normed, inverse, back * gain_out)
    branch = grad.astype(BF)
    put_halves(2048, tn(mixed, branch).astype(BF))
    mixed_grad = nt(branch, cross_out[...]).astype(BF).astype(F32)
    pieces = []
    pair_low = []
    for pair in range(HEADS // 2):
        at = slice(128 * pair, 128 * (pair + 1))
        value = values[:, at]
        key_turned = keys_turned[at, :]
        parts = []
        key_sum = None
        value_sum = None
        for odd in range(2):
            head = 2 * pair + odd
            given = jnp.where(low if odd == 0 else jnp.logical_not(low), mixed_grad[:, at], 0.0).astype(BF)
            chance = chances[head]
            chance_grad = nt(value, given)
            inner = jnp.sum(chance * chance_grad, axis=0, keepdims=True)
            score_grad = (chance * (chance_grad - inner)).astype(BF)
            parts.append(nn(key_turned, score_grad))
            key_part = nn(score_grad, masked[head])
            value_part = nn(chance.astype(BF), given)
            key_sum = key_part if key_sum is None else key_sum + key_part
            value_sum = value_part if value_sum is None else value_sum + value_part
        pair_low.append((key_sum.astype(BF), value_sum.astype(BF)))
        pieces.append(jnp.transpose(jnp.where(upper, parts[0], parts[1])) * SCALE)
    low_grad = jnp.concatenate(pieces, axis=1).astype(BF)
    back = nt(low_grad, query_weight[...])
    vectors[0:1, :] = jnp.sum(back * normed_two, axis=0, keepdims=True)
    vectors[1:2, :] = jnp.sum(back, axis=0, keepdims=True)
    vectors[4:8, :] = jnp.zeros((4, WIDTH), F32)
    grad = grad + norm_back(normed_two, inverse_two, back * gain)
    self_grad[...] = grad
    branch = grad.astype(BF)
    pack_heads(nt(branch, self_out[...]), message)
    put_halves(2304, tn(hidden, low_grad).astype(BF))
    put_halves(2560, tn(attended_low, branch).astype(BF))
    key_grad = jnp.concatenate([p[0] for p in pair_low], axis=1)
    value_grad = jnp.concatenate([p[1] for p in pair_low], axis=1)
    put_halves(2816, nn(every_turned[...], key_grad).astype(BF))
    pair_value[...] = nn(every_turned[...], value_grad).astype(BF)
    feed_pack[0, 3008:3072, :] = jnp.zeros((64, WIDTH), BF)
    feed_pack[1, 3008:3072, :] = jnp.zeros((64, WIDTH), BF)
    move(2048, 1024, 2048, 1)
    def feature_block(k, carry):
        rows = pl.ds(pl.multiple_of(256 * k, 256), 256)
        part = (nt(key_all[rows, :], pair_keys) + nt(value_all[rows, :], pair_values)).astype(BF)
        for i in range(8):
            for j in range(3):
                feature_part[8 * k + i, 32 * j : 32 * (j + 1), :] = part[
                    32 * i : 32 * (i + 1), 128 * j : 128 * (j + 1)
                ]
        return carry

    pair_keys, pair_values = pair_weight[:, :WIDTH], pair_weight[:, WIDTH:]
    key_all[...] = key_grad
    value_all[...] = value_grad
    lax.fori_loop(0, PATCHES // 256, feature_block, 0)
    for slot, rows in enumerate((2048, 1024)):
        for k in range(2):
            pltpu.make_async_copy(
                feed_pack.at[0, 0:rows], feed_keep.at[0:rows], semaphores.at[slot, k]
            ).wait()


def put_halves(place, keep, send, start, value):
    rows = value.shape[0] // 2
    put(place, keep, send, 0, slice(start, start + rows), value[:rows])
    put(place, keep, send, 1, slice(start, start + rows), value[rows:])


def attend_back_kernel(
    received, pairs_turned, attended, log_total, given, feature_part, message,
    masked_keys, pairs, queries, outer, outer_row, chances, score_grads, query_sum, turned,
):
    received = received.ready()
    gather_keys(received, masked_keys, pairs, queries, None)
    low = low_lanes(16)

    def unpack(k):
        piece = given[k].astype(F32)
        outer[pl.ds(pl.multiple_of(SHARE * k, 16), 16), :] = jnp.where(low, 0.0, half_turn(piece)).astype(BF)
        outer[pl.ds(pl.multiple_of(SHARE * k + 16, 16), 16), :] = jnp.where(low, 0.0, piece).astype(BF)
        message[k, 144:240, :] = feature_part[k]

    loop(PEERS, unpack, 4)
    attended = attended.ready()

    def inner(k):
        rows = block_of(k, 256)
        turned = jnp.transpose(outer[rows, :].astype(F32))[64:128, :]
        outer_row[:, rows] = jnp.broadcast_to(
            jnp.sum(turned * attended[:, rows], axis=0, keepdims=True), (8, 256)
        )

    loop(QUERIES // 256, inner)
    query_sum[...] = jnp.zeros_like(query_sum)
    pairs_turned, log_total = pairs_turned.ready(), log_total.ready()

    def chunk(turn, carry):
        at = pl.ds(pl.multiple_of(turn * BACK_KEYS, BACK_KEYS), BACK_KEYS)
        key = masked_keys[at, :]
        both = pairs[at, :]
        for k in range(QUERIES // BACK_ROWS):
            rows = slice(BACK_ROWS * k, BACK_ROWS * (k + 1))
            chance = jnp.exp(nt(key, queries[rows, :]) - log_total[0:1, rows])
            chance_grad = nt(both, outer[rows, :])
            chances[:, rows] = chance.astype(BF)
            score_grads[:, rows] = (chance * (chance_grad - outer_row[0:1, rows])).astype(BF)
        sums = nn(score_grads[...], queries[...])
        other = nn(chances[...], outer[...])
        sums = jnp.where(low_lanes(BACK_KEYS), sums, other).astype(BF)
        for k in range(BACK_KEYS // 128):
            message[turn * (BACK_KEYS // 128) + k, 0:128, :] = sums[128 * k : 128 * (k + 1), :]
        query_sum[...] += nn(pairs_turned[:, at], score_grads[...])
        return carry

    lax.fori_loop(0, TOKENS // BACK_KEYS, chunk, 0, unroll=UNROLL_C)
    turned[...] = jnp.transpose(query_sum[...]) * SCALE

    def pack(k):
        first = turned[pl.ds(pl.multiple_of(SHARE * k, 16), 16), :]
        second = turned[pl.ds(pl.multiple_of(SHARE * k + 16, 16), 16), :]
        message[k, 128:144, :] = jnp.where(low, first, half_turn(second)).astype(BF)

    loop(PEERS, pack, 4)


def finish_kernel(
    place, received, tokens, camera, modulation, self_grad, in_weight, vectors,
    pair_value, token_grad, feature_grad, keep, send,
):
    total = received[0, 144:240, :].astype(F32)
    for k in range(1, PEERS):
        total = total + received[k, 144:240, :].astype(F32)
    for j in range(3):
        feature_grad[:, 128 * j : 128 * (j + 1)] = total[32 * j : 32 * (j + 1), :]
    low = low_lanes(BLOCK)
    queries = []
    keys = []
    values = []
    for pair in range(HEADS // 2):
        sums = []
        for odd in range(2):
            head = 2 * pair + odd
            total = received[QUARTERS * head, 0:128, :].astype(F32)
            for quarter in range(1, QUARTERS):
                total = total + received[QUARTERS * head + quarter, 0:128, :].astype(F32)
            sums.append(total)
        keys.append(jnp.where(low, sums[0], half_turn(sums[1])))
        values.append(jnp.where(low, half_turn(sums[0]), sums[1]))
        low_half = low_lanes(16)
        pieces = []
        for quarter in range(QUARTERS):
            even = received[QUARTERS * (2 * pair) + quarter, 128:144, :].astype(F32)
            odd = received[QUARTERS * (2 * pair + 1) + quarter, 128:144, :].astype(F32)
            pieces.append(jnp.where(low_half, even, half_turn(odd)))
            pieces.append(jnp.where(low_half, half_turn(even), odd))
        queries.append(jnp.concatenate(pieces, axis=0))
    parts = [jnp.concatenate(p, axis=1).astype(BF) for p in (queries, keys, values)]
    normed, inverse = norm_parts(tokens[...].astype(F32))
    scale = 1.0 + modulation[0:1, :WIDTH]
    hidden = (normed * scale + modulation[0:1, WIDTH:]).astype(BF)
    back = jnp.zeros((BLOCK, WIDTH), F32)
    for k in range(3):
        at = slice(WIDTH * k, WIDTH * (k + 1))
        back = back + nt(parts[k], in_weight[:, at])
        put_halves(place, keep, send, 256 * k, tn(hidden, parts[k]).astype(BF))
    token_grad[...] = self_grad[...] + norm_back(normed, inverse, back * scale)
    scale_grad = jnp.sum(back * normed, axis=0, keepdims=True)
    shift_grad = jnp.sum(back, axis=0, keepdims=True)
    cam = camera[...].astype(F32)
    cam_act = cam * jax.nn.sigmoid(cam)
    row = lax.broadcasted_iota(jnp.int32, (32, WIDTH), 0)
    item = place[1]
    first = place[2] == 0
    small = jnp.where(row == item, scale_grad, 0.0)
    small = small + jnp.where(row == 4 + item, shift_grad, 0.0)
    small = small + jnp.where(jnp.logical_and(first, row == 8 + item), cam_act[:, :WIDTH], 0.0)
    small = small + jnp.where(jnp.logical_and(first, row == 12 + item), cam_act[:, WIDTH:], 0.0)
    small = small + jnp.where(row == 16, vectors[0:1, :], 0.0)
    small = small + jnp.where(row == 17, vectors[1:2, :], 0.0)
    small = small + jnp.where(row == 18, vectors[2:3, :], 0.0)
    small = small + jnp.where(row == 19, vectors[3:4, :], 0.0)
    put_halves(place, keep, send, 768, pair_value[...])
    keep[960:992, :] = small.astype(BF)
    send[960:992, :] = small.astype(BF)
    keep[992:1024, :] = jnp.zeros((32, WIDTH), BF)
    send[992:1024, :] = jnp.zeros((32, WIDTH), BF)


def sum_split_kernel(which, place, *refs):
    parts, pieces = refs[:-4], refs[-4:]
    rows = pieces[0].shape[0]
    for k in range(4):
        at = pl.ds(pl.multiple_of(lax.rem(place[which] + k, 4) * rows, rows), rows)
        total = parts[0][at, :].astype(F32)
        for part in parts[1:]:
            total = total + part[at, :].astype(F32)
        pieces[k][...] = total.astype(BF)


def halves_kernel(place, value, mine, other):
    rows = mine.shape[0]
    mine[...] = value[pl.ds(pl.multiple_of(place[0] * rows, rows), rows), :]
    other[...] = value[pl.ds(pl.multiple_of((1 - place[0]) * rows, rows), rows), :]


def sum_kernel(*refs):
    total = refs[0][...].astype(F32)
    for part in refs[1:-1]:
        total = total + part[...].astype(F32)
    refs[-1][...] = total.astype(BF)


def sum_pairs_kernel(first, second, third, fourth, out):
    rows = first.shape[0]
    out[0:rows, :] = (first[...].astype(F32) + second[...].astype(F32)).astype(BF)
    out[rows : 2 * rows, :] = (third[...].astype(F32) + fourth[...].astype(F32)).astype(BF)


def arrange_kernel(which, place, *refs):
    pieces, out = refs[:-1], refs[-1]
    rows = pieces[0].shape[0]
    for k in range(4):
        at = pl.ds(pl.multiple_of(lax.rem(place[which] + 4 - k, 4) * rows, rows), rows)
        out[at, :] = pieces[k][...]


def sum_far_kernel(far_pieces, out, pieces, semaphores):
    count = pieces.shape[0] // 4
    copies = []
    for k in range(4):
        at = slice(count * k, count * (k + 1))
        copies.append(pltpu.make_async_copy(far_pieces.at[at], pieces.at[at], semaphores.at[k]))
        copies[-1].start()
    total = None
    for k in range(4):
        copies[k].wait()
        for j in range(count * k, count * (k + 1)):
            piece = pieces[j].astype(F32)
            total = piece if total is None else total + piece
    out[...] = total.astype(BF)


def sum_pieces_kernel(pieces, *outs):
    total = pieces[0].astype(F32)
    for k in range(1, pieces.shape[0]):
        total = total + pieces[k].astype(F32)
    total = total.astype(BF)
    for out in outs:
        if len(out.shape) == 2:
            out[...] = total
        else:
            for k in range(out.shape[0]):
                out[k] = total


def write_halves(core, early, late, outs, buffers, semaphores):
    up_grad, down_grad, self_in, pair, self_out, cross_query, cross_out = outs
    up_part, down_part, in_part, pair_part, out_part, query_part, cross_part = buffers
    copies = []

    def send(part, target, slot):
        rows = part.shape[0]
        at = pl.ds(pl.multiple_of(core * rows, rows), rows)
        copies.append(pltpu.make_async_copy(part, target.at[at, :], semaphores.at[slot]))
        copies[-1].start()

    for k in range(4):
        up_part[:, 512 * k : 512 * (k + 1)] = early[256 * k : 256 * (k + 1), :].astype(F32)
    send(up_part, up_grad, 0)
    down_part[...] = early[1024:2048, :].astype(F32)
    send(down_part, down_grad, 1)
    for k in range(3):
        in_part[:, 512 * k : 512 * (k + 1)] = late[256 * k : 256 * (k + 1), :].astype(F32)
    send(in_part, self_in, 2)
    pair_part[:, :WIDTH] = early[2816:3008, :].astype(F32)
    pair_part[:, WIDTH:] = late[768:960, :].astype(F32)
    send(pair_part, pair, 3)
    out_part[...] = early[2560:2816, :].astype(F32)
    send(out_part, self_out, 4)
    query_part[...] = early[2304:2560, :].astype(F32)
    send(query_part, cross_query, 5)
    cross_part[...] = early[2048:2304, :].astype(F32)
    send(cross_part, cross_out, 6)
    return copies


def own_out_kernel(place, early, late, *refs):
    mod_weight, mod_bias, gain_two, offset_two, gain_three, offset_three = refs[7:13]
    small = late[960:992, :].astype(F32)
    grads = small[0:8, :]
    acts = small[8:16, :].astype(BF)
    head = lax.broadcasted_iota(jnp.int32, (8, WIDTH), 0) < 4
    turned = pltpu.roll(grads, 4, 0)
    mod_weight[:WIDTH, :WIDTH] = tn(acts, jnp.where(head, grads, 0.0).astype(BF))
    mod_weight[:WIDTH, WIDTH:] = tn(acts, jnp.where(head, turned, 0.0).astype(BF))
    mod_weight[WIDTH:, :WIDTH] = tn(acts, jnp.where(head, 0.0, turned).astype(BF))
    mod_weight[WIDTH:, WIDTH:] = tn(acts, jnp.where(head, 0.0, grads).astype(BF))
    mod_weight.send()
    gain_two[...] = small[16:17, :]
    offset_two[...] = small[17:18, :]
    gain_three[...] = small[18:19, :]
    offset_three[...] = small[19:20, :]
    mod_bias[:, :WIDTH] = jnp.sum(jnp.where(head, grads, 0.0), axis=0, keepdims=True)
    mod_bias[:, WIDTH:] = jnp.sum(jnp.where(head, 0.0, grads), axis=0, keepdims=True)
    for copy in write_halves(place[0], early, late, refs[:7], refs[13:20], refs[20]):
        copy.wait()


def other_out_kernel(place, early, late, *refs):
    for copy in write_halves(1 - place[0], early, late, refs[7:14], refs[14:21], refs[21]):
        copy.wait()


def index_of(x, y, z, core):
    return ((z % 2) * 2 + core) * 32 + (y * 4 + x) * 2 + z // 2


CHIPS = [(x, y, z) for x in range(4) for y in range(4) for z in range(4)]
SAME_CORE = [[index_of(*chip, core) for chip in CHIPS] for core in range(2)]
SAME_PLANE = [
    [index_of(x, y, z, core) for x in range(4) for y in range(4)] for z in range(4) for core in range(2)
]
OTHER_CORE = [
    (index_of(*chip, core), index_of(*chip, 1 - core)) for chip in CHIPS for core in range(2)
]


def shift_of(axis, step):
    moves = []
    for chip in CHIPS:
        there = list(chip)
        there[axis] = (there[axis] + step) % 4
        moves += [(index_of(*chip, core), index_of(*there, core)) for core in range(2)]
    return moves


SHIFTS = {(axis, step): shift_of(axis, step) for axis in range(3) for step in (1, 2, 3)}


def exchange(message):
    return lax.all_to_all(message, "seq", 0, 0, tiled=True)


def swap_cores(value):
    return lax.ppermute(value, AXES, OTHER_CORE)


def scatter_ring(pieces, axis):
    return (pieces[0],) + tuple(lax.ppermute(pieces[k], AXES, SHIFTS[axis, k]) for k in (1, 3, 2))


def gather_ring(piece, axis):
    came = {k: lax.ppermute(piece, AXES, SHIFTS[axis, k]) for k in (1, 3, 2)}
    return piece, came[1], came[2], came[3]


def sum_split(place, parts, axis):
    rows = parts[0].shape[0] // 4
    return call(
        functools.partial(sum_split_kernel, 3 + axis), (shape((rows, WIDTH), BF),) * 4, (place, *parts),
        traffic=4e5, smem=(0,),
    )


def sum_all(parts):
    return call(sum_kernel, shape(parts[0].shape, BF), parts, traffic=4e5)


def arrange(place, parts, axis):
    return call(
        functools.partial(arrange_kernel, 3 + axis), shape((4 * parts[0].shape[0], WIDTH), BF), (place, *parts),
        traffic=4e5, smem=(0,),
    )


def scatter_chips(value):
    rows = value.shape[0] // 64
    return lax.all_to_all(
        value.reshape(64, rows, WIDTH), AXES, 0, 0, tiled=True, axis_index_groups=SAME_CORE
    )


def in_one_step(always, work, *values):
    def nothing(*values):
        return jax.tree.map(lambda v: jnp.zeros(v.shape, v.dtype), jax.eval_shape(work, *values))

    return lax.cond(always, work, nothing, *values)


def body(
    tokens, camera, features, foreground, layout, modulation_weight, modulation_bias,
    self_in_weight, self_out_weight, cross_norm_gain, cross_norm_bias, cross_query_weight,
    cross_pair_weight, cross_out_weight, feed_norm_gain, feed_norm_bias, up_weight, down_weight,
    cotangent,
):
    tokens = tokens[0]
    features = features[0]
    cotangent = cotangent[0]
    row = lambda v: v.reshape(1, -1)
    step = functools.partial(in_one_step, layout[0, 0] >= 0)
    gain_two, offset_two = row(cross_norm_gain), row(cross_norm_bias)
    gain_three, offset_three = row(feed_norm_gain), row(feed_norm_bias)
    item, spot = lax.axis_index("batch"), lax.axis_index("seq")
    place = jnp.stack(
        [item & 1, item, spot, (spot >> 1) & 3, spot >> 3, (spot & 1) * 2 + (item >> 1)]
    ).astype(jnp.int32)

    message, modulation = call(
        prepare_kernel,
        (shape((PEERS, 240, 128), BF), shape((8, 1024))),
        (foreground, layout, tokens, features, camera, modulation_weight, modulation_bias, self_in_weight),
        flops=1e9, traffic=8e6, smem=(0, 1), late=(4, 5, 2, 7, 3), far_out=(0,), limit=57,
        scratch=(pltpu.VMEM((PEERS, 240, 128), BF), pltpu.SemaphoreType.DMA((HEADS,))),
    )
    received = exchange(message)
    message, attended_turned, log_total, pairs_turned = call(
        attend_kernel,
        (shape((PEERS, 16, 128), BF), shape((64, QUERIES)), shape((8, QUERIES)), shape((128, TOKENS), BF)),
        (received,),
        scratch=(
            pltpu.VMEM((TOKENS, 128), BF), pltpu.VMEM((QUERIES, 128), BF), pltpu.VMEM((TOKENS, ROWS), F32),
            pltpu.VMEM((128, QUERIES), F32), pltpu.VMEM((QUERIES, 128), F32),
        ),
        flops=9e9, traffic=4e6,
    )
    back = exchange(message)
    keys, values, keys_turned, values_turned, every_turned, kept = call(
        pairs_kernel,
        (
            shape((PATCHES, WIDTH), BF), shape((PATCHES, WIDTH), BF), shape((WIDTH, PATCHES), BF),
            shape((WIDTH, PATCHES), BF), shape((384, PATCHES), BF),
            shape((PEERS, 144, 128), BF),
        ),
        (received, cross_pair_weight),
        scratch=(pltpu.VMEM((PATCHES, 384), BF),),
        flops=3e9, traffic=8e6, late=(1,), away=(5, 0, 1, 2, 3, 4),
    )
    (
        block_out, early_keep, early_send, vectors, message, self_grad, feature_message, pair_value,
    ) = call(
        middle_kernel,
        (
            shape((BLOCK, WIDTH)), shape((3072, WIDTH), BF), shape((3072, WIDTH), BF), shape((8, WIDTH)),
            shape((PEERS, 16, 128), BF), shape((BLOCK, WIDTH)), shape((PEERS, 96, 128), BF), shape((384, WIDTH), BF),
        ),
        (
            place, back, tokens, keys, keys_turned, values, values_turned, self_out_weight, gain_two, offset_two,
            cross_query_weight, cross_out_weight, gain_three, offset_three, up_weight, down_weight, cotangent,
            every_turned, cross_pair_weight,
        ),
        scratch=(
            pltpu.VMEM((2, 3072, WIDTH), BF), pltpu.SemaphoreType.DMA((2, 2)), pltpu.VMEM((PATCHES, WIDTH), BF),
            pltpu.VMEM((PATCHES, WIDTH), BF), pltpu.VMEM((BLOCK, WIDTH), F32), pltpu.VMEM((BLOCK, WIDTH), F32),
        ),
        flops=1.6e10, traffic=2e7, smem=(0,), late=(7, 2, 10, 3, 6, 11, 14, 16, 15, 5, 4, 17, 18), limit=57,
        far_out=(1, 2),
    )

    def attend_back(message):
        given = exchange(message)
        total = sum_all((early_keep, swap_cores(early_send)))
        given, total = lax.optimization_barrier((given, total))
        pieces = scatter_chips(total)
        message = call(
            attend_back_kernel,
            shape((PEERS, 240, 128), BF),
            (kept, pairs_turned, attended_turned, log_total, given, feature_message),
            scratch=(
                pltpu.VMEM((TOKENS, 128), BF), pltpu.VMEM((TOKENS, 128), BF), pltpu.VMEM((QUERIES, 128), BF),
                pltpu.VMEM((QUERIES, 128), BF), pltpu.VMEM((8, QUERIES), F32),
                pltpu.VMEM((BACK_KEYS, QUERIES), BF), pltpu.VMEM((BACK_KEYS, QUERIES), BF),
                pltpu.VMEM((128, QUERIES), F32), pltpu.VMEM((QUERIES, 128), F32),
            ),
            flops=1.6e10, traffic=8e6, late=(0, 2, 1, 3),
        )
        return message, pieces

    message, pieces = step(attend_back, message)
    early = call(
        sum_far_kernel, shape((48, WIDTH), BF), (pieces,), traffic=3e6, far_in=(0,),
        scratch=(pltpu.VMEM(pieces.shape, BF), pltpu.SemaphoreType.DMA((4,))),
    )
    early = lax.all_gather(early, AXES, axis=0, tiled=True, axis_index_groups=SAME_CORE)

    def finish(message):
        returned = exchange(message)
        token_grad, feature_grad, keep, send = call(
            finish_kernel,
            (shape((BLOCK, WIDTH)), shape((32, 384)), shape((1024, WIDTH), BF), shape((1024, WIDTH), BF)),
            (
                place, returned, tokens, camera, modulation, self_grad, self_in_weight, vectors,
                pair_value,
            ),
            flops=3e9, traffic=8e6, smem=(0,), late=(2, 6, 4, 5),
        )
        pieces = scatter_chips(sum_all((keep, swap_cores(send))))
        total = call(sum_pieces_kernel, shape(pieces.shape, BF), (pieces,), traffic=2e6)
        late = lax.all_to_all(
            total, AXES, 0, 0, tiled=True, axis_index_groups=SAME_CORE
        ).reshape(1024, WIDTH)
        return token_grad, feature_grad, late

    token_grad, feature_grad, late = step(finish, message)
    early, late = lax.optimization_barrier((early, late))
    early_other, late_other = swap_cores(early), swap_cores(late)
    square = shape((WIDTH, WIDTH))
    vector = shape((1, WIDTH))
    grads = (shape((WIDTH, 2048)), shape((2048, WIDTH)), shape((WIDTH, 3 * WIDTH)), shape((384, 1024))) + (square,) * 3
    halves = tuple(pltpu.VMEM((g.shape[0] // 2, g.shape[1]), F32) for g in grads)
    halves += (pltpu.SemaphoreType.DMA((7,)),)
    *grads, mod_weight_grad, mod_bias_grad, gain_two_grad, offset_two_grad, gain_three_grad, offset_three_grad = call(
        own_out_kernel, grads + (shape((1024, 1024)), shape((1, 1024))) + (vector,) * 4, (place, early, late),
        scratch=halves, traffic=1.4e7, smem=(0,), late=(1,), away=(7,), far_out=tuple(range(7)), limit=57,
    )
    up_grad, down_grad, self_in_grad, pair_grad, self_out_grad, cross_query_grad, cross_out_grad = call(
        other_out_kernel,
        tuple(shape(g.shape) for g in grads),
        (place, early_other, late_other, *grads),
        scratch=halves, traffic=1.4e7, smem=(0,), far_in=tuple(range(3, 10)), far_out=tuple(range(7)),
        aliases={3 + k: k for k in range(7)},
    )
    return (
        block_out[None],
        token_grad[None],
        feature_grad[None],
        mod_weight_grad,
        mod_bias_grad[0],
        self_in_grad,
        self_out_grad,
        gain_two_grad[0],
        offset_two_grad[0],
        cross_query_grad,
        pair_grad,
        cross_out_grad,
        gain_three_grad[0],
        offset_three_grad[0],
        up_grad,
        down_grad,
    )


def solution(mesh):
    split = P("batch", "seq", None)
    in_specs = (
        (split, P("batch", None), split, P("batch", None), P("batch", "seq")) + (P(),) * 13 + (split,)
    )
    out_specs = (split,) * 3 + (P(),) * 13
    return jax.shard_map(body, mesh=mesh, in_specs=in_specs, out_specs=out_specs, check_vma=False)
```

profile of v0, /device:TPU:1, one launch (start us, length us, event | category | flops | bytes accessed | tf_op | source)
XLA Modules:
  0.0 278.7 jit_solution(5045376184278051859)
XLA Ops:
  7.9 5.2 %shard_map.306 = (bf16[32,240,128]{2,1,0:T(8,128)(2,1)}, f32[8,1024]{1,0:T(8,128)S(1)}) custom-call(s32[1,8]{1,0:T(1,128)} %refs_0_.1, s32[1,1]{1,0:T(1,128)S(6)} %copy.59.refs_1_, bf16[128,512]{1,0:T(8,128)(2,1)} %bitcast.24, bf16[32,384]{1,0:T(8,128)(2,1)} %bitcast.28, bf16[1,1024]{1,0:T(2,128)(2,1)} %refs_4_.1, bf16[1024,1024]{1,0:T(8,128)(2,1)} %refs_5_.1, ...), custom_call_target="tpu_custom_call" | custom-call | flops 1000000000 | bytes 8000000 | tf_op jit(solution)/shard_map/pallas_call | solution.py:130
  13.1 11.2 %all-to-all-start.5 = ((bf16[32,240,128]{2,1,0:T(8,128)(2,1)}), bf16[32,240,128]{2,1,0:T(8,128)(2,1)S(1)}, u32[]{:S(2)}, u32[]{:S(2)}) async-start(bf16[32,240,128]{2,1,0:T(8,128)(2,1)} %get-tuple-element.122), calls=%async_computation.5 | async-start | bytes 3932160 | tf_op jit(solution)/shard_map/all_to_all | solution.py:784
  26.8 25.8 %all-to-all-done.5.refs_0_ = bf16[32,240,128]{2,1,0:T(8,128)(2,1)S(1)} async-done(((bf16[32,240,128]{2,1,0:T(8,128)(2,1)}), bf16[32,240,128]{2,1,0:T(8,128)(2,1)S(1)}, u32[]{:S(2)}, u32[]{:S(2)}) %all-to-all-start.5) | async-done | bytes 1966112 | tf_op jit(solution)/shard_map/all_to_all | solution.py:784
  52.6 9.1 %shard_map.307 = (bf16[32,16,128]{2,1,0:T(8,128)(2,1)}, f32[64,1024]{1,0:T(8,128)}, f32[8,1024]{1,0:T(8,128)S(1)}, bf16[128,4096]{1,0:T(8,128)(2,1)}) custom-call(bf16[32,240,128]{2,1,0:T(8,128)(2,1)S(1)} %all-to-all-done.5.refs_0_), custom_call_target="tpu_custom_call" | custom-call | flops 8999999488 | bytes 4000000 | tf_op jit(solution)/shard_map/pallas_call | solution.py:130
  61.7 5.0 %all-to-all-start.6 = ((bf16[32,16,128]{2,1,0:T(8,128)(2,1)}), bf16[32,16,128]{2,1,0:T(8,128)(2,1)S(1)}, u32[]{:S(2)}, u32[]{:S(2)}) async-start(bf16[32,16,128]{2,1,0:T(8,128)(2,1)} %get-tuple-element.123), calls=%async_computation.6 | async-start | bytes 262144 | tf_op jit(solution)/shard_map/all_to_all | solution.py:784
  67.0 2.8 shard_map.308
  69.8 1.0 copy-done.1
  70.7 1.0 copy-done.2
  71.7 1.0 copy-done.3
  72.7 1.0 copy-done.4
  74.6 1.3 all-to-all-done.6.refs_1_
  76.5 18.9 %shard_map.309 = (f32[128,512]{1,0:T(8,128)}, bf16[3072,512]{1,0:T(8,128)(2,1)}, bf16[3072,512]{1,0:T(8,128)(2,1)}, f32[8,512]{1,0:T(8,128)S(1)}, bf16[32,16,128...) custom-call(s32[6]{0:T(128)S(1)} %stack.27.refs_0_, ...), custom_call_target="tpu_custom_call" | custom-call | flops 16000000000 | bytes 20000000 | tf_op jit(solution)/shard_map/pallas_call | solution.py:130
  95.5 63.4 %conditional.2 = (bf16[32,240,128]{2,1,0:T(8,128)(2,1)}, bf16[64,48,512]{2,1,0:T(8,128)(2,1)}) conditional(s32[]{:T(128)} %bitcast.15, () %tuple.31, (bf16[32,16,128]{2,1,0:T(8,128)(2,1)}, bf16[3072,512]{1,0:T(8,128)(2,1)}, bf16[3072,512]{1,0:T(8,128)(2,1)}, bf16[32,144,128]{2,1,0:T(8,128)(2,1)}, bf16[128,4096]{1,0:T(8,128)(2,1)}, ...), branch_computations={%region_0.0_spmd, %region_1.0_spmd} | conditional | flops 16000000000 | bytes 42872140 | solution.py:830
  95.5 2.8 %collective-permute-start = (bf16[3072,512]{1,0:T(8,128)(2,1)}, bf16[3072,512]{1,0:T(8,128)(2,1)S(1)}, u32[]{:S(2)}, u32[]{:S(2)}) collective-permute-start(bf16[3072,512]{1,0:T(8,128)(2,1)} %get-tuple-element.42), channel_id=1, source_target_pairs={{0,32},{32,0},{64,96},{96,64},{1,33},{33,1},{65,97},{97,65},{8,40}... | collective-permute-start | bytes 9437192 | tf_op jit(solution)/shard_map/cond/branch_1_fun/ppermute | solution.py:788
  98.3 7.1 %all-to-all-start = ((bf16[32,16,128]{2,1,0:T(8,128)(2,1)}), bf16[32,16,128]{2,1,0:T(8,128)(2,1)S(1)}, u32[]{:S(2)}, u32[]{:S(2)}) async-start(bf16[32,16,128]{2,1,0:T(8,128)(2,1)} %get-tuple-element.40), calls=%async_computation | async-start | bytes 262144 | tf_op jit(solution)/shard_map/cond/branch_1_fun/all_to_all | solution.py:784
  105.4 4.4 %branch_1_fun.5 = bf16[3072,512]{1,0:T(8,128)(2,1)} custom-call(bf16[3072,512]{1,0:T(8,128)(2,1)} %get-tuple-element.41.refs_0_, bf16[3072,512]{1,0:T(8,128)(2,1)S(1)} %collective-permute-done.refs_1_), custom_call_target="tpu_custom_call" | custom-call | bytes 400000 | tf_op jit(solution)/shard_map/cond/branch_1_fun/pallas_call | solution.py:130
  109.8 5.0 %all-to-all-done.refs_4_ = bf16[32,16,128]{2,1,0:T(8,128)(2,1)S(1)} async-done(((bf16[32,16,128]{2,1,0:T(8,128)(2,1)}), bf16[32,16,128]{2,1,0:T(8,128)(2,1)S(1)}, u32[]{:S(2)}, u32[]{:S(2)}) %all-to-all-start) | async-done | bytes 131104 | tf_op jit(solution)/shard_map/cond/branch_1_fun/all_to_all | solution.py:784
  114.8 5.8 %all-to-all-start.1 = ((bf16[64,48,512]{2,1,0:T(8,128)(2,1)}), bf16[64,48,512]{2,1,0:T(8,128)(2,1)}, u32[]{:S(2)}, u32[]{:S(2)}) async-start(bf16[64,48,512]{2,1,0:T(8,128)(2,1)} %bitcast), calls=%async_computation.1 | async-start | bytes 6291456 | tf_op jit(solution)/shard_map/cond/branch_1_fun/all_to_all | solution.py:821
  120.7 14.7 %branch_1_fun.6 = bf16[32,240,128]{2,1,0:T(8,128)(2,1)} custom-call(bf16[32,144,128]{2,1,0:T(8,128)(2,1)S(1)} %copy-done.14, bf16[128,4096]{1,0:T(8,128)(2,1)S(1)} %copy-done.17, f32[64,1024]{1,0:T(8,128)} %get-tuple-element.38.refs_2_, f32[8,1024]{1,0:T(8,128)S(1)} %get-tuple-element.39.refs_3_, bf16[32,16,128]{2,1,0:T(8,128)(2,1)S(1)} %all-to-all-done.refs_4_, ...), custom_call_target="tpu_custom_call" | custom-call | flops 16000000000 | bytes 8000000 | tf_op jit(solution)/shard_map/cond/branch_1_fun/pallas_call | solution.py:130
  135.3 23.5 %all-to-all-done.1 = bf16[64,48,512]{2,1,0:T(8,128)(2,1)} async-done(((bf16[64,48,512]{2,1,0:T(8,128)(2,1)}), bf16[64,48,512]{2,1,0:T(8,128)(2,1)}, u32[]{:S(2)}, u32[]{:S(2)}) %all-to-all-start.1) | async-done | bytes 3145760 | tf_op jit(solution)/shard_map/cond/branch_1_fun/all_to_all | solution.py:821
  158.9 2.8 shard_map.310
  161.7 96.6 %conditional.3 = (bf16[1024,512]{1,0:T(8,128)(2,1)S(1)}, f32[1,128,512]{2,1,0:T(8,128)}, f32[1,32,384]{2,1,0:T(8,128)}) conditional(s32[]{:T(128)} %bitcast.15, () %tuple.30, (bf16[32,240,128]{2,1,0:T(8,128)(2,1)}, s32[6]{0:T(128)S(1)}, bf16[128,512]{1,0:T(8,128)(2,1)S(1)}, bf16[1,1024]{1,0:T(2,128)(2,1)S(1)}, f32[8,1024]{1,0:T(8,128)S(1)}, ...), branch_computations={%region_2.0_spmd, %region_3.0_spmd} | conditional | flops 3000000000 | bytes 22720832 | solution.py:830
  161.8 36.1 %all_to_all.30.refs_1_ = bf16[32,240,128]{2,1,0:T(8,128)(2,1)S(1)} all-to-all(bf16[32,240,128]{2,1,0:T(8,128)(2,1)} %get-tuple-element.47), channel_id=1, replica_groups=mesh['batch'=4,'seq'=32] {'seq'}, dimensions={0} | all-to-all | bytes 3932160 | tf_op jit(solution)/shard_map/cond/branch_1_fun/all_to_all | solution.py:784
  197.8 3.9 %branch_1_fun.7 = (f32[128,512]{1,0:T(8,128)}, f32[32,384]{1,0:T(8,128)}, bf16[1024,512]{1,0:T(8,128)(2,1)S(1)}, bf16[1024,512]{1,0:T(8,128)(2,1)S(1)}) custom-call(s32[6]{0:T(128)S(1)} %get-tuple-element.46.refs_0_, bf16[32,240,128]{2,1,0:T(8,128)(2,1)S(1)} %all_to_all.30.refs_1_, bf16[128,512]{1,0:T(8,128)(2,1)S(1)} %get-tuple-element.48.refs_2_, ...), custom_call_target="tpu_custom_call" | custom-call | flops 3000000000 | bytes 8000000 | tf_op jit(solution)/shard_map/cond/branch_1_fun/pallas_call | solution.py:130
  201.8 2.9 %collective-permute-start.1 = (bf16[1024,512]{1,0:T(8,128)(2,1)S(1)}, bf16[1024,512]{1,0:T(8,128)(2,1)S(1)}, u32[]{:S(2)}, u32[]{:S(2)}) collective-permute-start(bf16[1024,512]{1,0:T(8,128)(2,1)S(1)} %get-tuple-element.56), channel_id=1, source_target_pairs={{0,32},{32,0},{64,96},{96,64},{1,33},{33,1},{65,97},{97,65},{8,40}... | collective-permute-start | bytes 3145736 | tf_op jit(solution)/shard_map/cond/branch_1_fun/ppermute | solution.py:788
  204.6 2.3 collective-permute-done.1.refs_1_
  207.2 21.5 %all_to_all.31.refs_0_ = bf16[64,16,512]{2,1,0:T(8,128)(2,1)S(1)} all-to-all(bf16[64,16,512]{2,1,0:T(8,128)(2,1)S(1)} %bitcast.21), channel_id=1, replica_groups={{0,64,1,65,8,72,9,73,16,80,17,81,24,88,25,89,2,66,3,67,10,74,11,75,18,8..., dimensions={0} | all-to-all | bytes 2097152 | tf_op jit(solution)/shard_map/cond/branch_1_fun/all_to_all | solution.py:821
  228.9 29.4 %all_to_all.32 = bf16[64,16,512]{2,1,0:T(8,128)(2,1)S(1)} all-to-all(bf16[64,16,512]{2,1,0:T(8,128)(2,1)S(1)} %branch_1_fun.9), channel_id=1, replica_groups={{0,64,1,65,8,72,9,73,16,80,17,81,24,88,25,89,2,66,3,67,10,74,11,75,18,8..., dimensions={0} | all-to-all | bytes 2097152 | tf_op jit(solution)/shard_map/cond/branch_1_fun/all_to_all | solution.py:941
  258.3 1.2 all-gather.2.cloned.1.call-done.refs_1_
  259.5 1.4 collective-permute-start.2
  260.9 6.8 %shard_map.311 = (f32[512,2048]{1,0:T(8,128)}, f32[2048,512]{1,0:T(8,128)}, f32[512,1536]{1,0:T(8,128)}, f32[384,1024]{1,0:T(8,128)}, f32[512,512]{1,0:T(8,128)}...) custom-call(s32[6]{0:T(128)S(1)} %stack.27.refs_0_, ...), custom_call_target="tpu_custom_call" | custom-call | bytes 14000000 | tf_op jit(solution)/shard_map/pallas_call | solution.py:130
  267.9 3.9 %shard_map.312 = (f32[512,2048]{1,0:T(8,128)}, f32[2048,512]{1,0:T(8,128)}, f32[512,1536]{1,0:T(8,128)}, f32[384,1024]{1,0:T(8,128)}, f32[512,512]{1,0:T(8,128)}...) custom-call(s32[6]{0:T(128)S(1)} %stack.27.refs_0_, ...), custom_call_target="tpu_custom_call", output_to_operand_aliasing={{0}: (3, {}), {1}: (4, {}), {2}: (5, {}), {3}: (6, {}), {4}... | custom-call | bytes 14000000 | tf_op jit(solution)/shard_map/pallas_call | solution.py:130
  (47 shorter events, 4.9 us)
Async XLA Ops:
  7.8 16.5 %copy-start.10 = (bf16[512]{0:T(512)(128)(2,1)S(1)}, bf16[512]{0:T(512)(128)(2,1)}, u32[]{:S(2)}) copy-start(bf16[512]{0:T(512)(128)(2,1)} %param.32) | copy-start | bytes 3076
  7.8 17.1 %copy-start.11 = (bf16[512]{0:T(512)(128)(2,1)S(1)}, bf16[512]{0:T(512)(128)(2,1)}, u32[]{:S(2)}) copy-start(bf16[512]{0:T(512)(128)(2,1)} %param.33) | copy-start | bytes 3076
  7.8 17.7 %copy-start.12 = (bf16[512]{0:T(512)(128)(2,1)S(1)}, bf16[512]{0:T(512)(128)(2,1)}, u32[]{:S(2)}) copy-start(bf16[512]{0:T(512)(128)(2,1)} %param.37) | copy-start | bytes 3076
  7.9 18.2 %copy-start.13 = (bf16[512]{0:T(512)(128)(2,1)S(1)}, bf16[512]{0:T(512)(128)(2,1)}, u32[]{:S(2)}) copy-start(bf16[512]{0:T(512)(128)(2,1)} %param.38) | copy-start | bytes 3076
  13.1 39.5 %all-to-all-start.5 = ((bf16[32,240,128]{2,1,0:T(8,128)(2,1)}), bf16[32,240,128]{2,1,0:T(8,128)(2,1)S(1)}, u32[]{:S(2)}, u32[]{:S(2)}) async-start(bf16[32,240,128]{2,1,0:T(8,128)(2,1)} %get-tuple-element.122), calls=%async_computation.5 | async-start | bytes 3932160 | tf_op jit(solution)/shard_map/all_to_all | solution.py:784
  26.8 40.2 %copy-start = (bf16[384,1024]{1,0:T(8,128)(2,1)S(1)}, bf16[384,1024]{1,0:T(8,128)(2,1)}, u32[]{:S(2)}) copy-start(bf16[384,1024]{1,0:T(8,128)(2,1)} %refs_18_.1) | copy-start | bytes 2359300
  61.7 14.1 %all-to-all-start.6 = ((bf16[32,16,128]{2,1,0:T(8,128)(2,1)}), bf16[32,16,128]{2,1,0:T(8,128)(2,1)S(1)}, u32[]{:S(2)}, u32[]{:S(2)}) async-start(bf16[32,16,128]{2,1,0:T(8,128)(2,1)} %get-tuple-element.123), calls=%async_computation.6 | async-start | bytes 262144 | tf_op jit(solution)/shard_map/all_to_all | solution.py:784
  66.8 9.7 %copy-start.7 = (bf16[1,128,512]{2,1,0:T(8,128)(2,1)S(1)}, bf16[1,128,512]{2,1,0:T(8,128)(2,1)}, u32[]{:S(2)}) copy-start(bf16[1,128,512]{2,1,0:T(8,128)(2,1)} %param.23) | copy-start | bytes 393220
  66.8 192.7 %all-gather.2.cloned.1.call-start = ((), (), s32[]{:S(2)}) async-start(), calls=%async_computation.7 | async-start | bytes 3194880 | tf_op jit(solution)/shard_map/all_gather | solution.py:926
  69.8 1.0 copy-start.1
  70.7 1.0 copy-start.2
  71.7 1.0 copy-start.3
  72.7 1.0 copy-start.4
  73.7 0.9 copy-start.5
  75.9 0.6 copy-start.8
  95.5 9.9 %collective-permute-start = (bf16[3072,512]{1,0:T(8,128)(2,1)}, bf16[3072,512]{1,0:T(8,128)(2,1)S(1)}, u32[]{:S(2)}, u32[]{:S(2)}) collective-permute-start(bf16[3072,512]{1,0:T(8,128)(2,1)} %get-tuple-element.42), channel_id=1, source_target_pairs={{0,32},{32,0},{64,96},{96,64},{1,33},{33,1},{65,97},{97,65},{8,40}... | collective-permute-start | bytes 9437192 | tf_op jit(solution)/shard_map/cond/branch_1_fun/ppermute | solution.py:788
  98.3 16.5 %all-to-all-start = ((bf16[32,16,128]{2,1,0:T(8,128)(2,1)}), bf16[32,16,128]{2,1,0:T(8,128)(2,1)S(1)}, u32[]{:S(2)}, u32[]{:S(2)}) async-start(bf16[32,16,128]{2,1,0:T(8,128)(2,1)} %get-tuple-element.40), calls=%async_computation | async-start | bytes 262144 | tf_op jit(solution)/shard_map/cond/branch_1_fun/all_to_all | solution.py:784
  114.8 5.9 %copy-start.14 = (bf16[32,144,128]{2,1,0:T(8,128)(2,1)S(1)}, bf16[32,144,128]{2,1,0:T(8,128)(2,1)}, u32[]{:S(2)}) copy-start(bf16[32,144,128]{2,1,0:T(8,128)(2,1)} %get-tuple-element.36.refs_0_) | copy-start | bytes 3538948 | tf_op jit(solution)/shard_map/cond
  114.8 5.9 %copy-start.17 = (bf16[128,4096]{1,0:T(8,128)(2,1)S(1)}, bf16[128,4096]{1,0:T(8,128)(2,1)}, u32[]{:S(2)}) copy-start(bf16[128,4096]{1,0:T(8,128)(2,1)} %get-tuple-element.37.refs_1_) | copy-start | bytes 3145732 | tf_op jit(solution)/shard_map/cond
  114.8 5.9 %copy-start.18 = (bf16[32,96,128]{2,1,0:T(8,128)(2,1)S(1)}, bf16[32,96,128]{2,1,0:T(8,128)(2,1)}, u32[]{:S(2)}) copy-start(bf16[32,96,128]{2,1,0:T(8,128)(2,1)} %get-tuple-element.44.refs_5_) | copy-start | bytes 2359300 | tf_op jit(solution)/shard_map/cond
  114.8 44.1 %all-to-all-start.1 = ((bf16[64,48,512]{2,1,0:T(8,128)(2,1)}), bf16[64,48,512]{2,1,0:T(8,128)(2,1)}, u32[]{:S(2)}, u32[]{:S(2)}) async-start(bf16[64,48,512]{2,1,0:T(8,128)(2,1)} %bitcast), calls=%async_computation.1 | async-start | bytes 6291456 | tf_op jit(solution)/shard_map/cond/branch_1_fun/all_to_all | solution.py:821
  158.9 2.8 %copy-start.6 = (bf16[512,1536]{1,0:T(8,128)(2,1)S(1)}, bf16[512,1536]{1,0:T(8,128)(2,1)}, u32[]{:S(2)}) copy-start(bf16[512,1536]{1,0:T(8,128)(2,1)} %refs_7_.2) | copy-start | bytes 4718596
  158.9 2.8 %copy-start.9 = (bf16[1,1024]{1,0:T(2,128)(2,1)S(1)}, bf16[1,1024]{1,0:T(2,128)(2,1)}, u32[]{:S(2)}) copy-start(bf16[1,1024]{1,0:T(2,128)(2,1)} %refs_4_.1) | copy-start | bytes 6148
  158.9 2.8 %copy-start.15 = (bf16[384,512]{1,0:T(8,128)(2,1)S(1)}, bf16[384,512]{1,0:T(8,128)(2,1)}, u32[]{:S(2)}) copy-start(bf16[384,512]{1,0:T(8,128)(2,1)} %get-tuple-element.142) | copy-start | bytes 1179652
  158.9 2.8 %copy-start.16 = (f32[128,512]{1,0:T(8,128)S(1)}, f32[128,512]{1,0:T(8,128)}, u32[]{:S(2)}) copy-start(f32[128,512]{1,0:T(8,128)} %get-tuple-element.140) | copy-start | bytes 786436
  201.8 5.1 %collective-permute-start.1 = (bf16[1024,512]{1,0:T(8,128)(2,1)S(1)}, bf16[1024,512]{1,0:T(8,128)(2,1)S(1)}, u32[]{:S(2)}, u32[]{:S(2)}) collective-permute-start(bf16[1024,512]{1,0:T(8,128)(2,1)S(1)} %get-tuple-element.56), channel_id=1, source_target_pairs={{0,32},{32,0},{64,96},{96,64},{1,33},{33,1},{65,97},{97,65},{8,40}... | collective-permute-start | bytes 3145736 | tf_op jit(solution)/shard_map/cond/branch_1_fun/ppermute | solution.py:788
  259.5 8.4 %collective-permute-start.2 = (bf16[3072,512]{1,0:T(8,128)(2,1)}, bf16[3072,512]{1,0:T(8,128)(2,1)S(1)}, u32[]{:S(2)}, u32[]{:S(2)}) collective-permute-start(bf16[3072,512]{1,0:T(8,128)(2,1)} %all-gather.2.cloned.1.call-done.refs_1_), channel_id=1, source_target_pairs={{0,32},{32,0},{64,96},{96,64},{1,33},{33,1},{65,97},{97,65},{8,40}... | collective-permute-start | bytes 9437192 | tf_op jit(solution)/shard_map/ppermute | solution.py:788
  260.9 6.8 %collective-permute-start.3 = (bf16[1024,512]{1,0:T(8,128)(2,1)S(1)}, bf16[1024,512]{1,0:T(8,128)(2,1)S(1)}, u32[]{:S(2)}, u32[]{:S(2)}) collective-permute-start(bf16[1024,512]{1,0:T(8,128)(2,1)S(1)} %get-tuple-element.148.refs_2_), channel_id=1, source_target_pairs={{0,32},{32,0},{64,96},{96,64},{1,33},{33,1},{65,97},{97,65},{8,40}... | collective-permute-start | bytes 3145736 | tf_op jit(solution)/shard_map/ppermute | solution.py:788
Sparse Core Ops, SparseCore 0:
  161.8 97.6 all-gather.1
where the time goes:
time: 279 us
  blocking collectives  87 us (31%)
  Pallas kernels  73 us (26%)
  waiting for transfers between devices  59.3 us (21%)
  starting transfers between devices  36.5 us (13%)
  between operations  14.9 us (5%)
  local copies, waits for them, and re-layouts  7.88 us (3%)
    pallas_call x12, Pallas kernels, call(): pl.pallas_call(whole, out_shape=out_shape, in_specs=[scalar if k in smem...  73 us
    all_to_all x1, blocking collectives, exchange(): return lax.all_to_all(message, 'seq', 0, 0, tiled=True)  36.1 us
    all_to_all x3, waiting for transfers between devices, exchange(): return lax.all_to_all(message, 'seq', 0, 0, tiled=True)  32.1 us
    all_to_all x1, blocking collectives, finish(): lax.all_to_all(total, AXES, 0, 0, tiled=True, axis_index_groups=SAME_CORE)  29.4 us
    all_to_all x1, waiting for transfers between devices, scatter_chips(): lax.all_to_all(value.reshape(64, rows, WIDTH), AXES, 0, 0, tiled=True, ax...  23.5 us
    all_to_all x3, starting transfers between devices, exchange(): return lax.all_to_all(message, 'seq', 0, 0, tiled=True)  23.3 us
    all_to_all x1, blocking collectives, scatter_chips(): lax.all_to_all(value.reshape(64, rows, WIDTH), AXES, 0, 0, tiled=True, ax...  21.5 us
    ppermute x4, starting transfers between devices, swap_cores(): return lax.ppermute(value, AXES, OTHER_CORE)  7.13 us
  transfers between devices with their start and end apart: 9, of which 7 were waited for; matrix products, arithmetic and copies ran while one was open for 1% of the time, Pallas kernels for 12%

commit v1 on v0

--- a/solution.py
+++ b/solution.py
@@ -149,9 +149,6 @@
     foreground, layout, tokens, features, camera, mod_weight, mod_bias, in_weight,
     far_message, modulation, message, semaphores,
 ):
-    for to in range(PEERS):
-        for k in range(3):
-            message[to, 144 + 32 * k : 176 + 32 * k, :] = features[:, 128 * k : 128 * (k + 1)]
     cam = camera[...].astype(F32)
     cam_act = (cam * jax.nn.sigmoid(cam)).astype(BF)
     mod = nn(jnp.broadcast_to(cam_act, (16, cam_act.shape[1])), mod_weight[...])[0:8]
@@ -190,6 +187,8 @@
                 to = QUARTERS * head + quarter
                 message[to, 0:128, :] = both
                 top = SHARE * quarter
+                for k in range(3):
+                    message[to, 144 + 32 * k : 176 + 32 * k, :] = features[:, 128 * k : 128 * (k + 1)]
                 message[to, 128:144, :] = jnp.where(
                     low_half, first[top : top + 16], second[top + 16 : top + 32]
                 ).astype(BF)
@@ -667,22 +666,6 @@
         out[at, :] = pieces[k][...]
 
 
-def sum_far_kernel(far_pieces, out, pieces, semaphores):
-    count = pieces.shape[0] // 4
-    copies = []
-    for k in range(4):
-        at = slice(count * k, count * (k + 1))
-        copies.append(pltpu.make_async_copy(far_pieces.at[at], pieces.at[at], semaphores.at[k]))
-        copies[-1].start()
-    total = None
-    for k in range(4):
-        copies[k].wait()
-        for j in range(count * k, count * (k + 1)):
-            piece = pieces[j].astype(F32)
-            total = piece if total is None else total + piece
-    out[...] = total.astype(BF)
-
-
 def sum_pieces_kernel(pieces, *outs):
     total = pieces[0].astype(F32)
     for k in range(1, pieces.shape[0]):
@@ -852,7 +835,7 @@
         prepare_kernel,
         (shape((PEERS, 240, 128), BF), shape((8, 1024))),
         (foreground, layout, tokens, features, camera, modulation_weight, modulation_bias, self_in_weight),
-        flops=1e9, traffic=8e6, smem=(0, 1), late=(4, 5, 2, 7, 3), far_out=(0,), limit=57,
+        flops=1e9, traffic=8e6, smem=(0, 1), late=(4, 5, 2, 7, 3, 6), far_out=(0,), limit=57,
         scratch=(pltpu.VMEM((PEERS, 240, 128), BF), pltpu.SemaphoreType.DMA((HEADS,))),
     )
     received = exchange(message)
@@ -895,7 +878,8 @@
             pltpu.VMEM((2, 3072, WIDTH), BF), pltpu.SemaphoreType.DMA((2, 2)), pltpu.VMEM((PATCHES, WIDTH), BF),
             pltpu.VMEM((PATCHES, WIDTH), BF), pltpu.VMEM((BLOCK, WIDTH), F32), pltpu.VMEM((BLOCK, WIDTH), F32),
         ),
-        flops=1.6e10, traffic=2e7, smem=(0,), late=(7, 2, 10, 3, 6, 11, 14, 16, 15, 5, 4, 17, 18), limit=57,
+        flops=1.6e10, traffic=2e7, smem=(0,), late=(1, 7, 2, 8, 9, 10, 3, 6, 11, 12, 13, 14, 16, 15, 5, 4, 17, 18),
+        limit=57,
         far_out=(1, 2),
     )
 
@@ -916,13 +900,10 @@
             ),
             flops=1.6e10, traffic=8e6, late=(0, 2, 1, 3),
         )
-        return message, pieces
-
-    message, pieces = step(attend_back, message)
-    early = call(
-        sum_far_kernel, shape((48, WIDTH), BF), (pieces,), traffic=3e6, far_in=(0,),
-        scratch=(pltpu.VMEM(pieces.shape, BF), pltpu.SemaphoreType.DMA((4,))),
-    )
+        message, pieces = lax.optimization_barrier((message, pieces))
+        return message, call(sum_pieces_kernel, shape((48, WIDTH), BF), (pieces,), traffic=3e6)
+
+    message, early = step(attend_back, message)
     early = lax.all_gather(early, AXES, axis=0, tiled=True, axis_index_groups=SAME_CORE)
 
     def finish(message):

time: 279 us -> 277 us (level)
    unnamed x32 -> x28, local copies, waits for them, and re-layouts: 5.46 us -> 6.07 us
where the time goes in v1:
time: 277 us; the launch traced here: 276 us
  blocking collectives  86.8 us (31%)
  Pallas kernels  70.3 us (25%)
  waiting for transfers between devices  57.7 us (21%)
  starting transfers between devices  35.9 us (13%)
  between operations  14.9 us (5%)
  local copies, waits for them, and re-layouts  10.2 us (4%)
    pallas_call x12, Pallas kernels, call(): pl.pallas_call(whole, out_shape=out_shape, in_specs=[scalar if k in smem...  70.3 us
    all_to_all x1, blocking collectives, exchange(): return lax.all_to_all(message, 'seq', 0, 0, tiled=True)  35.9 us
    all_to_all x3, waiting for transfers between devices, exchange(): return lax.all_to_all(message, 'seq', 0, 0, tiled=True)  32.2 us
    all_to_all x1, blocking collectives, finish(): lax.all_to_all(total, AXES, 0, 0, tiled=True, axis_index_groups=SAME_CORE)  29 us
    all_to_all x3, starting transfers between devices, exchange(): return lax.all_to_all(message, 'seq', 0, 0, tiled=True)  23.3 us
    all_to_all x1, waiting for transfers between devices, scatter_chips(): lax.all_to_all(value.reshape(64, rows, WIDTH), AXES, 0, 0, tiled=True, ax...  22.1 us
    all_to_all x1, blocking collectives, scatter_chips(): lax.all_to_all(value.reshape(64, rows, WIDTH), AXES, 0, 0, tiled=True, ax...  21.8 us
    ppermute x4, starting transfers between devices, swap_cores(): return lax.ppermute(value, AXES, OTHER_CORE)  7.45 us
  transfers between devices with their start and end apart: 9, of which 7 were waited for; matrix products, arithmetic and copies ran while one was open for 1% of the time, Pallas kernels for 12%

profile of v1, /device:TPU:1, one launch (start us, length us, event | category | flops | bytes accessed | tf_op | source)
XLA Modules:
  0.0 276.0 jit_solution(15035308227428567079)
XLA Ops:
  7.9 4.9 %shard_map.306 = (bf16[32,240,128]{2,1,0:T(8,128)(2,1)}, f32[8,1024]{1,0:T(8,128)S(1)}) custom-call(s32[1,8]{1,0:T(1,128)} %refs_0_.1, s32[1,1]{1,0:T(1,128)S(6)} %copy.59.refs_1_, bf16[128,512]{1,0:T(8,128)(2,1)} %bitcast.25, bf16[32,384]{1,0:T(8,128)(2,1)} %bitcast.29, bf16[1,1024]{1,0:T(2,128)(2,1)} %refs_4_.1, bf16[1024,1024]{1,0:T(8,128)(2,1)} %refs_5_.1, ...), custom_call_target="tpu_custom_call" | custom-call | flops 1000000000 | bytes 8000000 | tf_op jit(solution)/shard_map/pallas_call | solution.py:130
  12.7 11.2 %all-to-all-start.5 = ((bf16[32,240,128]{2,1,0:T(8,128)(2,1)}), bf16[32,240,128]{2,1,0:T(8,128)(2,1)S(1)}, u32[]{:S(2)}, u32[]{:S(2)}) async-start(bf16[32,240,128]{2,1,0:T(8,128)(2,1)} %get-tuple-element.124), calls=%async_computation.5 | async-start | bytes 3932160 | tf_op jit(solution)/shard_map/all_to_all | solution.py:767
  26.4 25.8 %all-to-all-done.5.refs_0_ = bf16[32,240,128]{2,1,0:T(8,128)(2,1)S(1)} async-done(((bf16[32,240,128]{2,1,0:T(8,128)(2,1)}), bf16[32,240,128]{2,1,0:T(8,128)(2,1)S(1)}, u32[]{:S(2)}, u32[]{:S(2)}) %all-to-all-start.5) | async-done | bytes 1966112 | tf_op jit(solution)/shard_map/all_to_all | solution.py:767
  52.2 9.1 %shard_map.307 = (bf16[32,16,128]{2,1,0:T(8,128)(2,1)}, f32[64,1024]{1,0:T(8,128)}, f32[8,1024]{1,0:T(8,128)S(1)}, bf16[128,4096]{1,0:T(8,128)(2,1)}) custom-call(bf16[32,240,128]{2,1,0:T(8,128)(2,1)S(1)} %all-to-all-done.5.refs_0_), custom_call_target="tpu_custom_call" | custom-call | flops 8999999488 | bytes 4000000 | tf_op jit(solution)/shard_map/pallas_call | solution.py:130
  61.3 5.0 %all-to-all-start.6 = ((bf16[32,16,128]{2,1,0:T(8,128)(2,1)}), bf16[32,16,128]{2,1,0:T(8,128)(2,1)S(1)}, u32[]{:S(2)}, u32[]{:S(2)}) async-start(bf16[32,16,128]{2,1,0:T(8,128)(2,1)} %get-tuple-element.125), calls=%async_computation.6 | async-start | bytes 262144 | tf_op jit(solution)/shard_map/all_to_all | solution.py:767
  66.6 2.8 shard_map.308
  69.4 1.0 copy-done.2
  70.4 1.0 copy-done.3
  71.3 1.0 copy-done.4
  72.3 1.0 copy-done.5
  73.3 0.9 copy-done.6
  74.2 1.3 all-to-all-done.6.refs_1_
  76.1 18.7 %shard_map.309 = (f32[128,512]{1,0:T(8,128)}, bf16[3072,512]{1,0:T(8,128)(2,1)}, bf16[3072,512]{1,0:T(8,128)(2,1)}, f32[8,512]{1,0:T(8,128)S(1)}, bf16[32,16,128...) custom-call(s32[6]{0:T(128)S(1)} %stack.27.refs_0_, ...), custom_call_target="tpu_custom_call" | custom-call | flops 16000000000 | bytes 20000000 | tf_op jit(solution)/shard_map/pallas_call | solution.py:130
  94.8 63.7 %conditional.2 = (bf16[32,240,128]{2,1,0:T(8,128)(2,1)}, bf16[48,512]{1,0:T(8,128)(2,1)S(1)}) conditional(s32[]{:T(128)} %bitcast.15, () %tuple.32, (bf16[32,16,128]{2,1,0:T(8,128)(2,1)}, bf16[3072,512]{1,0:T(8,128)(2,1)}, bf16[3072,512]{1,0:T(8,128)(2,1)}, bf16[32,144,128]{2,1,0:T(8,128)(2,1)}, bf16[128,4096]{1,0:T(8,128)(2,1)}, ...), branch_computations={%region_0.0_spmd, %region_1.0_spmd} | conditional | flops 16000000000 | bytes 46396372 | solution.py:813
  94.8 2.8 %collective-permute-start = (bf16[3072,512]{1,0:T(8,128)(2,1)}, bf16[3072,512]{1,0:T(8,128)(2,1)S(1)}, u32[]{:S(2)}, u32[]{:S(2)}) collective-permute-start(bf16[3072,512]{1,0:T(8,128)(2,1)} %get-tuple-element.42), channel_id=1, source_target_pairs={{0,32},{32,0},{64,96},{96,64},{1,33},{33,1},{65,97},{97,65},{8,40}... | collective-permute-start | bytes 9437192 | tf_op jit(solution)/shard_map/cond/branch_1_fun/ppermute | solution.py:771
  97.7 7.1 %all-to-all-start = ((bf16[32,16,128]{2,1,0:T(8,128)(2,1)}), bf16[32,16,128]{2,1,0:T(8,128)(2,1)S(1)}, u32[]{:S(2)}, u32[]{:S(2)}) async-start(bf16[32,16,128]{2,1,0:T(8,128)(2,1)} %get-tuple-element.40), calls=%async_computation | async-start | bytes 262144 | tf_op jit(solution)/shard_map/cond/branch_1_fun/all_to_all | solution.py:767
  104.8 2.6 branch_1_fun.6
  107.4 1.7 copy-done
  109.1 5.1 %all-to-all-done.refs_4_ = bf16[32,16,128]{2,1,0:T(8,128)(2,1)S(1)} async-done(((bf16[32,16,128]{2,1,0:T(8,128)(2,1)}), bf16[32,16,128]{2,1,0:T(8,128)(2,1)S(1)}, u32[]{:S(2)}, u32[]{:S(2)}) %all-to-all-start) | async-done | bytes 131104 | tf_op jit(solution)/shard_map/cond/branch_1_fun/all_to_all | solution.py:767
  114.1 4.9 %all-to-all-start.1 = ((bf16[64,48,512]{2,1,0:T(8,128)(2,1)}), bf16[64,48,512]{2,1,0:T(8,128)(2,1)S(1)}, u32[]{:S(2)}, u32[]{:S(2)}) async-start(bf16[64,48,512]{2,1,0:T(8,128)(2,1)} %bitcast.21), calls=%async_computation.1 | async-start | bytes 6291456 | tf_op jit(solution)/shard_map/cond/branch_1_fun/all_to_all | solution.py:804
  119.1 16.7 %branch_1_fun.7 = bf16[32,240,128]{2,1,0:T(8,128)(2,1)} custom-call(bf16[32,144,128]{2,1,0:T(8,128)(2,1)} %get-tuple-element.36.refs_0_, bf16[128,4096]{1,0:T(8,128)(2,1)} %get-tuple-element.37.refs_1_, f32[64,1024]{1,0:T(8,128)} %get-tuple-element.38.refs_2_, f32[8,1024]{1,0:T(8,128)S(1)} %get-tuple-element.39.refs_3_, ...), custom_call_target="tpu_custom_call" | custom-call | flops 16000000000 | bytes 8000000 | tf_op jit(solution)/shard_map/cond/branch_1_fun/pallas_call | solution.py:130
  135.8 22.1 %all-to-all-done.1.refs_0_ = bf16[64,48,512]{2,1,0:T(8,128)(2,1)S(1)} async-done(((bf16[64,48,512]{2,1,0:T(8,128)(2,1)}), bf16[64,48,512]{2,1,0:T(8,128)(2,1)S(1)}, u32[]{:S(2)}, u32[]{:S(2)}) %all-to-all-start.1) | async-done | bytes 3145760 | tf_op jit(solution)/shard_map/cond/branch_1_fun/all_to_all | solution.py:804
  159.2 96.3 %conditional.3 = (bf16[1024,512]{1,0:T(8,128)(2,1)S(1)}, f32[1,128,512]{2,1,0:T(8,128)}, f32[1,32,384]{2,1,0:T(8,128)}) conditional(s32[]{:T(128)} %bitcast.15, () %tuple.31, (bf16[32,240,128]{2,1,0:T(8,128)(2,1)}, s32[6]{0:T(128)S(1)}, bf16[128,512]{1,0:T(8,128)(2,1)S(1)}, bf16[1,1024]{1,0:T(2,128)(2,1)S(1)}, f32[8,1024]{1,0:T(8,128)S(1)}, ...), branch_computations={%region_2.0_spmd, %region_3.0_spmd} | conditional | flops 3000000000 | bytes 31633812 | solution.py:813
  159.3 35.9 %all_to_all.30.refs_1_ = bf16[32,240,128]{2,1,0:T(8,128)(2,1)S(1)} all-to-all(bf16[32,240,128]{2,1,0:T(8,128)(2,1)} %get-tuple-element.49), channel_id=1, replica_groups=mesh['batch'=4,'seq'=32] {'seq'}, dimensions={0} | all-to-all | bytes 3932160 | tf_op jit(solution)/shard_map/cond/branch_1_fun/all_to_all | solution.py:767
  195.2 3.9 %branch_1_fun.9 = (f32[128,512]{1,0:T(8,128)}, f32[32,384]{1,0:T(8,128)}, bf16[1024,512]{1,0:T(8,128)(2,1)S(1)}, bf16[1024,512]{1,0:T(8,128)(2,1)S(1)}) custom-call(s32[6]{0:T(128)S(1)} %get-tuple-element.48.refs_0_, bf16[32,240,128]{2,1,0:T(8,128)(2,1)S(1)} %all_to_all.30.refs_1_, bf16[128,512]{1,0:T(8,128)(2,1)S(1)} %get-tuple-element.50.refs_2_, ...), custom_call_target="tpu_custom_call" | custom-call | flops 3000000000 | bytes 8000000 | tf_op jit(solution)/shard_map/cond/branch_1_fun/pallas_call | solution.py:130
  199.2 2.7 collective-permute-start.1
  201.9 2.3 collective-permute-done.1.refs_1_
  204.4 21.8 %all_to_all.31.refs_0_ = bf16[64,16,512]{2,1,0:T(8,128)(2,1)S(1)} all-to-all(bf16[64,16,512]{2,1,0:T(8,128)(2,1)S(1)} %bitcast.22), channel_id=1, replica_groups={{0,64,1,65,8,72,9,73,16,80,17,81,24,88,25,89,2,66,3,67,10,74,11,75,18,8..., dimensions={0} | all-to-all | bytes 2097152 | tf_op jit(solution)/shard_map/cond/branch_1_fun/all_to_all | solution.py:804
  226.5 29.0 %all_to_all.32 = bf16[64,16,512]{2,1,0:T(8,128)(2,1)S(1)} all-to-all(bf16[64,16,512]{2,1,0:T(8,128)(2,1)S(1)} %branch_1_fun.11), channel_id=1, replica_groups={{0,64,1,65,8,72,9,73,16,80,17,81,24,88,25,89,2,66,3,67,10,74,11,75,18,8..., dimensions={0} | all-to-all | bytes 2097152 | tf_op jit(solution)/shard_map/cond/branch_1_fun/all_to_all | solution.py:922
  256.4 1.9 collective-permute-start.2
  258.2 6.8 %shard_map.310 = (f32[512,2048]{1,0:T(8,128)}, f32[2048,512]{1,0:T(8,128)}, f32[512,1536]{1,0:T(8,128)}, f32[384,1024]{1,0:T(8,128)}, f32[512,512]{1,0:T(8,128)}...) custom-call(s32[6]{0:T(128)S(1)} %stack.27.refs_0_, ...), custom_call_target="tpu_custom_call" | custom-call | bytes 14000000 | tf_op jit(solution)/shard_map/pallas_call | solution.py:130
  265.2 3.9 %shard_map.311 = (f32[512,2048]{1,0:T(8,128)}, f32[2048,512]{1,0:T(8,128)}, f32[512,1536]{1,0:T(8,128)}, f32[384,1024]{1,0:T(8,128)}, f32[512,512]{1,0:T(8,128)}...) custom-call(s32[6]{0:T(128)S(1)} %stack.27.refs_0_, ...), custom_call_target="tpu_custom_call", output_to_operand_aliasing={{0}: (3, {}), {1}: (4, {}), {2}: (5, {}), {3}: (6, {}), {4}... | custom-call | bytes 14000000 | tf_op jit(solution)/shard_map/pallas_call | solution.py:130
  (45 shorter events, 5.9 us)
Async XLA Ops:
  7.8 16.1 %copy-start.12 = (bf16[512]{0:T(512)(128)(2,1)S(1)}, bf16[512]{0:T(512)(128)(2,1)}, u32[]{:S(2)}) copy-start(bf16[512]{0:T(512)(128)(2,1)} %param.32) | copy-start | bytes 3076
  7.8 16.7 %copy-start.13 = (bf16[512]{0:T(512)(128)(2,1)S(1)}, bf16[512]{0:T(512)(128)(2,1)}, u32[]{:S(2)}) copy-start(bf16[512]{0:T(512)(128)(2,1)} %param.33) | copy-start | bytes 3076
  7.8 17.3 %copy-start.14 = (bf16[512]{0:T(512)(128)(2,1)S(1)}, bf16[512]{0:T(512)(128)(2,1)}, u32[]{:S(2)}) copy-start(bf16[512]{0:T(512)(128)(2,1)} %param.37) | copy-start | bytes 3076
  7.9 17.9 %copy-start.15 = (bf16[512]{0:T(512)(128)(2,1)S(1)}, bf16[512]{0:T(512)(128)(2,1)}, u32[]{:S(2)}) copy-start(bf16[512]{0:T(512)(128)(2,1)} %param.38) | copy-start | bytes 3076
  12.7 39.5 %all-to-all-start.5 = ((bf16[32,240,128]{2,1,0:T(8,128)(2,1)}), bf16[32,240,128]{2,1,0:T(8,128)(2,1)S(1)}, u32[]{:S(2)}, u32[]{:S(2)}) async-start(bf16[32,240,128]{2,1,0:T(8,128)(2,1)} %get-tuple-element.124), calls=%async_computation.5 | async-start | bytes 3932160 | tf_op jit(solution)/shard_map/all_to_all | solution.py:767
  26.4 40.2 %copy-start.1 = (bf16[384,1024]{1,0:T(8,128)(2,1)S(1)}, bf16[384,1024]{1,0:T(8,128)(2,1)}, u32[]{:S(2)}) copy-start(bf16[384,1024]{1,0:T(8,128)(2,1)} %refs_18_.1) | copy-start | bytes 2359300
  61.3 14.1 %all-to-all-start.6 = ((bf16[32,16,128]{2,1,0:T(8,128)(2,1)}), bf16[32,16,128]{2,1,0:T(8,128)(2,1)S(1)}, u32[]{:S(2)}, u32[]{:S(2)}) async-start(bf16[32,16,128]{2,1,0:T(8,128)(2,1)} %get-tuple-element.125), calls=%async_computation.6 | async-start | bytes 262144 | tf_op jit(solution)/shard_map/all_to_all | solution.py:767
  66.4 9.8 %copy-start.9 = (bf16[1,128,512]{2,1,0:T(8,128)(2,1)S(1)}, bf16[1,128,512]{2,1,0:T(8,128)(2,1)}, u32[]{:S(2)}) copy-start(bf16[1,128,512]{2,1,0:T(8,128)(2,1)} %param.23) | copy-start | bytes 393220
  66.4 190.0 %all-gather.2.cloned.1.call-start = ((), (), s32[]{:S(2)}) async-start(), calls=%async_computation.7 | async-start | bytes 3194880 | tf_op jit(solution)/shard_map/all_gather | solution.py:907
  69.4 1.0 copy-start.2
  70.4 1.0 copy-start.3
  71.3 1.0 copy-start.4
  72.3 1.0 copy-start.5
  73.3 0.9 copy-start.6
  75.5 0.7 copy-start.10
  94.8 64.4 %copy-start.11 = (bf16[1,1024]{1,0:T(2,128)(2,1)S(1)}, bf16[1,1024]{1,0:T(2,128)(2,1)}, u32[]{:S(2)}) copy-start(bf16[1,1024]{1,0:T(2,128)(2,1)} %refs_4_.1) | copy-start | bytes 6148
  94.8 9.9 %collective-permute-start = (bf16[3072,512]{1,0:T(8,128)(2,1)}, bf16[3072,512]{1,0:T(8,128)(2,1)S(1)}, u32[]{:S(2)}, u32[]{:S(2)}) collective-permute-start(bf16[3072,512]{1,0:T(8,128)(2,1)} %get-tuple-element.42), channel_id=1, source_target_pairs={{0,32},{32,0},{64,96},{96,64},{1,33},{33,1},{65,97},{97,65},{8,40}... | collective-permute-start | bytes 9437192 | tf_op jit(solution)/shard_map/cond/branch_1_fun/ppermute | solution.py:771
  97.7 16.5 %all-to-all-start = ((bf16[32,16,128]{2,1,0:T(8,128)(2,1)}), bf16[32,16,128]{2,1,0:T(8,128)(2,1)S(1)}, u32[]{:S(2)}, u32[]{:S(2)}) async-start(bf16[32,16,128]{2,1,0:T(8,128)(2,1)} %get-tuple-element.40), calls=%async_computation | async-start | bytes 262144 | tf_op jit(solution)/shard_map/cond/branch_1_fun/all_to_all | solution.py:767
  107.4 1.7 copy-start
  114.1 43.8 %all-to-all-start.1 = ((bf16[64,48,512]{2,1,0:T(8,128)(2,1)}), bf16[64,48,512]{2,1,0:T(8,128)(2,1)S(1)}, u32[]{:S(2)}, u32[]{:S(2)}) async-start(bf16[64,48,512]{2,1,0:T(8,128)(2,1)} %bitcast.21), calls=%async_computation.1 | async-start | bytes 6291456 | tf_op jit(solution)/shard_map/cond/branch_1_fun/all_to_all | solution.py:804
  158.6 0.6 copy-start.8
  159.2 36.0 %copy-start.7 = (bf16[512,1536]{1,0:T(8,128)(2,1)S(1)}, bf16[512,1536]{1,0:T(8,128)(2,1)}, u32[]{:S(2)}) copy-start(bf16[512,1536]{1,0:T(8,128)(2,1)} %get-tuple-element.54.refs_6_) | copy-start | bytes 4718596 | tf_op jit(solution)/shard_map/cond
  159.2 36.0 %copy-start.16 = (bf16[384,512]{1,0:T(8,128)(2,1)S(1)}, bf16[384,512]{1,0:T(8,128)(2,1)}, u32[]{:S(2)}) copy-start(bf16[384,512]{1,0:T(8,128)(2,1)} %get-tuple-element.56.refs_8_) | copy-start | bytes 1179652 | tf_op jit(solution)/shard_map/cond
  159.3 36.0 %copy-start.17 = (f32[128,512]{1,0:T(8,128)S(1)}, f32[128,512]{1,0:T(8,128)}, u32[]{:S(2)}) copy-start(f32[128,512]{1,0:T(8,128)} %get-tuple-element.53.refs_5_) | copy-start | bytes 786436 | tf_op jit(solution)/shard_map/cond
  199.2 5.0 %collective-permute-start.1 = (bf16[1024,512]{1,0:T(8,128)(2,1)S(1)}, bf16[1024,512]{1,0:T(8,128)(2,1)S(1)}, u32[]{:S(2)}, u32[]{:S(2)}) collective-permute-start(bf16[1024,512]{1,0:T(8,128)(2,1)S(1)} %get-tuple-element.58), channel_id=1, source_target_pairs={{0,32},{32,0},{64,96},{96,64},{1,33},{33,1},{65,97},{97,65},{8,40}... | collective-permute-start | bytes 3145736 | tf_op jit(solution)/shard_map/cond/branch_1_fun/ppermute | solution.py:771
  256.4 8.9 %collective-permute-start.2 = (bf16[3072,512]{1,0:T(8,128)(2,1)}, bf16[3072,512]{1,0:T(8,128)(2,1)S(1)}, u32[]{:S(2)}, u32[]{:S(2)}) collective-permute-start(bf16[3072,512]{1,0:T(8,128)(2,1)} %all-gather.2.cloned.1.call-done.refs_1_), channel_id=1, source_target_pairs={{0,32},{32,0},{64,96},{96,64},{1,33},{33,1},{65,97},{97,65},{8,40}... | collective-permute-start | bytes 9437192 | tf_op jit(solution)/shard_map/ppermute | solution.py:771
  258.2 6.8 %collective-permute-start.3 = (bf16[1024,512]{1,0:T(8,128)(2,1)S(1)}, bf16[1024,512]{1,0:T(8,128)(2,1)S(1)}, u32[]{:S(2)}, u32[]{:S(2)}) collective-permute-start(bf16[1024,512]{1,0:T(8,128)(2,1)S(1)} %get-tuple-element.150.refs_2_), channel_id=1, source_target_pairs={{0,32},{32,0},{64,96},{96,64},{1,33},{33,1},{65,97},{97,65},{8,40}... | collective-permute-start | bytes 3145736 | tf_op jit(solution)/shard_map/ppermute | solution.py:771
Sparse Core Ops, SparseCore 0:
  159.3 96.9 all-gather.1

commit v2 on v1

--- a/solution.py
+++ b/solution.py
@@ -239,7 +239,7 @@
 
 KEYS = 512
 ROWS = 1024
-UNROLL_A = 2
+UNROLL_A = 4
 UNROLL_B = 4
 UNROLL_C = 1
 BACK_KEYS = 1024

time: 277 us -> 276 us (level)
  no operation moved by 1% of the time
where the time goes in v2:
time: 276 us
  blocking collectives  86.8 us (31%)
  Pallas kernels  69.9 us (25%)
  waiting for transfers between devices  57.6 us (21%)
  starting transfers between devices  35.9 us (13%)
  between operations  14.9 us (5%)
  local copies, waits for them, and re-layouts  10.2 us (4%)
    pallas_call x12, Pallas kernels, call(): pl.pallas_call(whole, out_shape=out_shape, in_specs=[scalar if k in smem...  69.9 us
    all_to_all x1, blocking collectives, exchange(): return lax.all_to_all(message, 'seq', 0, 0, tiled=True)  35.9 us
    all_to_all x3, waiting for transfers between devices, exchange(): return lax.all_to_all(message, 'seq', 0, 0, tiled=True)  32.2 us
    all_to_all x1, blocking collectives, finish(): lax.all_to_all(total, AXES, 0, 0, tiled=True, axis_index_groups=SAME_CORE)  29 us
    all_to_all x3, starting transfers between devices, exchange(): return lax.all_to_all(message, 'seq', 0, 0, tiled=True)  23.3 us
    all_to_all x1, waiting for transfers between devices, scatter_chips(): lax.all_to_all(value.reshape(64, rows, WIDTH), AXES, 0, 0, tiled=True, ax...  22.1 us
    all_to_all x1, blocking collectives, scatter_chips(): lax.all_to_all(value.reshape(64, rows, WIDTH), AXES, 0, 0, tiled=True, ax...  21.8 us
    ppermute x4, starting transfers between devices, swap_cores(): return lax.ppermute(value, AXES, OTHER_CORE)  7.45 us
  transfers between devices with their start and end apart: 9, of which 7 were waited for; matrix products, arithmetic and copies ran while one was open for 1% of the time, Pallas kernels for 12%

profile of v2, /device:TPU:1, one launch (start us, length us, event | category | flops | bytes accessed | tf_op | source)
XLA Modules:
  0.0 275.6 jit_solution(17802371348965691573)
XLA Ops:
  7.9 4.9 %shard_map.306 = (bf16[32,240,128]{2,1,0:T(8,128)(2,1)}, f32[8,1024]{1,0:T(8,128)S(1)}) custom-call(s32[1,8]{1,0:T(1,128)} %refs_0_.1, s32[1,1]{1,0:T(1,128)S(6)} %copy.59.refs_1_, bf16[128,512]{1,0:T(8,128)(2,1)} %bitcast.25, bf16[32,384]{1,0:T(8,128)(2,1)} %bitcast.29, bf16[1,1024]{1,0:T(2,128)(2,1)} %refs_4_.1, bf16[1024,1024]{1,0:T(8,128)(2,1)} %refs_5_.1, ...), custom_call_target="tpu_custom_call" | custom-call | flops 1000000000 | bytes 8000000 | tf_op jit(solution)/shard_map/pallas_call | solution.py:130
  12.7 11.2 %all-to-all-start.5 = ((bf16[32,240,128]{2,1,0:T(8,128)(2,1)}), bf16[32,240,128]{2,1,0:T(8,128)(2,1)S(1)}, u32[]{:S(2)}, u32[]{:S(2)}) async-start(bf16[32,240,128]{2,1,0:T(8,128)(2,1)} %get-tuple-element.124), calls=%async_computation.5 | async-start | bytes 3932160 | tf_op jit(solution)/shard_map/all_to_all | solution.py:767
  26.4 25.8 %all-to-all-done.5.refs_0_ = bf16[32,240,128]{2,1,0:T(8,128)(2,1)S(1)} async-done(((bf16[32,240,128]{2,1,0:T(8,128)(2,1)}), bf16[32,240,128]{2,1,0:T(8,128)(2,1)S(1)}, u32[]{:S(2)}, u32[]{:S(2)}) %all-to-all-start.5) | async-done | bytes 1966112 | tf_op jit(solution)/shard_map/all_to_all | solution.py:767
  52.2 8.7 %shard_map.307 = (bf16[32,16,128]{2,1,0:T(8,128)(2,1)}, f32[64,1024]{1,0:T(8,128)}, f32[8,1024]{1,0:T(8,128)S(1)}, bf16[128,4096]{1,0:T(8,128)(2,1)}) custom-call(bf16[32,240,128]{2,1,0:T(8,128)(2,1)S(1)} %all-to-all-done.5.refs_0_), custom_call_target="tpu_custom_call" | custom-call | flops 8999999488 | bytes 4000000 | tf_op jit(solution)/shard_map/pallas_call | solution.py:130
  61.0 5.0 %all-to-all-start.6 = ((bf16[32,16,128]{2,1,0:T(8,128)(2,1)}), bf16[32,16,128]{2,1,0:T(8,128)(2,1)S(1)}, u32[]{:S(2)}, u32[]{:S(2)}) async-start(bf16[32,16,128]{2,1,0:T(8,128)(2,1)} %get-tuple-element.125), calls=%async_computation.6 | async-start | bytes 262144 | tf_op jit(solution)/shard_map/all_to_all | solution.py:767
  66.2 2.8 %shard_map.308 = (bf16[1024,512]{1,0:T(8,128)(2,1)S(1)}, bf16[1024,512]{1,0:T(8,128)(2,1)S(1)}, bf16[512,1024]{1,0:T(8,128)(2,1)S(1)}, bf16[512,1024]{1,0:T(8,12...) custom-call(bf16[32,240,128]{2,1,0:T(8,128)(2,1)S(1)} %all-to-all-done.5.refs_0_, ...), custom_call_target="tpu_custom_call" | custom-call | flops 3000000000 | bytes 8000000 | tf_op jit(solution)/shard_map/pallas_call | solution.py:130
  69.0 1.0 copy-done.2
  70.0 1.0 copy-done.3
  71.0 1.0 copy-done.4
  71.9 1.0 copy-done.5
  72.9 0.9 copy-done.6
  73.8 1.3 all-to-all-done.6.refs_1_
  75.8 18.7 %shard_map.309 = (f32[128,512]{1,0:T(8,128)}, bf16[3072,512]{1,0:T(8,128)(2,1)}, bf16[3072,512]{1,0:T(8,128)(2,1)}, f32[8,512]{1,0:T(8,128)S(1)}, bf16[32,16,128...) custom-call(s32[6]{0:T(128)S(1)} %stack.27.refs_0_, ...), custom_call_target="tpu_custom_call" | custom-call | flops 16000000000 | bytes 20000000 | tf_op jit(solution)/shard_map/pallas_call | solution.py:130
  94.4 63.7 %conditional.2 = (bf16[32,240,128]{2,1,0:T(8,128)(2,1)}, bf16[48,512]{1,0:T(8,128)(2,1)S(1)}) conditional(s32[]{:T(128)} %bitcast.15, () %tuple.32, (bf16[32,16,128]{2,1,0:T(8,128)(2,1)}, bf16[3072,512]{1,0:T(8,128)(2,1)}, bf16[3072,512]{1,0:T(8,128)(2,1)}, bf16[32,144,128]{2,1,0:T(8,128)(2,1)}, bf16[128,4096]{1,0:T(8,128)(2,1)}, ...), branch_computations={%region_0.0_spmd, %region_1.0_spmd} | conditional | flops 16000000000 | bytes 46396372 | solution.py:813
  94.5 2.8 %collective-permute-start = (bf16[3072,512]{1,0:T(8,128)(2,1)}, bf16[3072,512]{1,0:T(8,128)(2,1)S(1)}, u32[]{:S(2)}, u32[]{:S(2)}) collective-permute-start(bf16[3072,512]{1,0:T(8,128)(2,1)} %get-tuple-element.42), channel_id=1, source_target_pairs={{0,32},{32,0},{64,96},{96,64},{1,33},{33,1},{65,97},{97,65},{8,40}... | collective-permute-start | bytes 9437192 | tf_op jit(solution)/shard_map/cond/branch_1_fun/ppermute | solution.py:771
  97.3 7.1 %all-to-all-start = ((bf16[32,16,128]{2,1,0:T(8,128)(2,1)}), bf16[32,16,128]{2,1,0:T(8,128)(2,1)S(1)}, u32[]{:S(2)}, u32[]{:S(2)}) async-start(bf16[32,16,128]{2,1,0:T(8,128)(2,1)} %get-tuple-element.40), calls=%async_computation | async-start | bytes 262144 | tf_op jit(solution)/shard_map/cond/branch_1_fun/all_to_all | solution.py:767
  104.4 2.6 branch_1_fun.6
  107.0 1.7 copy-done
  108.7 5.1 %all-to-all-done.refs_4_ = bf16[32,16,128]{2,1,0:T(8,128)(2,1)S(1)} async-done(((bf16[32,16,128]{2,1,0:T(8,128)(2,1)}), bf16[32,16,128]{2,1,0:T(8,128)(2,1)S(1)}, u32[]{:S(2)}, u32[]{:S(2)}) %all-to-all-start) | async-done | bytes 131104 | tf_op jit(solution)/shard_map/cond/branch_1_fun/all_to_all | solution.py:767
  113.8 4.9 %all-to-all-start.1 = ((bf16[64,48,512]{2,1,0:T(8,128)(2,1)}), bf16[64,48,512]{2,1,0:T(8,128)(2,1)S(1)}, u32[]{:S(2)}, u32[]{:S(2)}) async-start(bf16[64,48,512]{2,1,0:T(8,128)(2,1)} %bitcast.21), calls=%async_computation.1 | async-start | bytes 6291456 | tf_op jit(solution)/shard_map/cond/branch_1_fun/all_to_all | solution.py:804
  118.7 16.7 %branch_1_fun.7 = bf16[32,240,128]{2,1,0:T(8,128)(2,1)} custom-call(bf16[32,144,128]{2,1,0:T(8,128)(2,1)} %get-tuple-element.36.refs_0_, bf16[128,4096]{1,0:T(8,128)(2,1)} %get-tuple-element.37.refs_1_, f32[64,1024]{1,0:T(8,128)} %get-tuple-element.38.refs_2_, f32[8,1024]{1,0:T(8,128)S(1)} %get-tuple-element.39.refs_3_, ...), custom_call_target="tpu_custom_call" | custom-call | flops 16000000000 | bytes 8000000 | tf_op jit(solution)/shard_map/cond/branch_1_fun/pallas_call | solution.py:130
  135.4 22.1 %all-to-all-done.1.refs_0_ = bf16[64,48,512]{2,1,0:T(8,128)(2,1)S(1)} async-done(((bf16[64,48,512]{2,1,0:T(8,128)(2,1)}), bf16[64,48,512]{2,1,0:T(8,128)(2,1)S(1)}, u32[]{:S(2)}, u32[]{:S(2)}) %all-to-all-start.1) | async-done | bytes 3145760 | tf_op jit(solution)/shard_map/cond/branch_1_fun/all_to_all | solution.py:804
  158.8 96.3 %conditional.3 = (bf16[1024,512]{1,0:T(8,128)(2,1)S(1)}, f32[1,128,512]{2,1,0:T(8,128)}, f32[1,32,384]{2,1,0:T(8,128)}) conditional(s32[]{:T(128)} %bitcast.15, () %tuple.31, (bf16[32,240,128]{2,1,0:T(8,128)(2,1)}, s32[6]{0:T(128)S(1)}, bf16[128,512]{1,0:T(8,128)(2,1)S(1)}, bf16[1,1024]{1,0:T(2,128)(2,1)S(1)}, f32[8,1024]{1,0:T(8,128)S(1)}, ...), branch_computations={%region_2.0_spmd, %region_3.0_spmd} | conditional | flops 3000000000 | bytes 31633812 | solution.py:813
  158.9 35.9 %all_to_all.30.refs_1_ = bf16[32,240,128]{2,1,0:T(8,128)(2,1)S(1)} all-to-all(bf16[32,240,128]{2,1,0:T(8,128)(2,1)} %get-tuple-element.49), channel_id=1, replica_groups=mesh['batch'=4,'seq'=32] {'seq'}, dimensions={0} | all-to-all | bytes 3932160 | tf_op jit(solution)/shard_map/cond/branch_1_fun/all_to_all | solution.py:767
  194.8 3.9 %branch_1_fun.9 = (f32[128,512]{1,0:T(8,128)}, f32[32,384]{1,0:T(8,128)}, bf16[1024,512]{1,0:T(8,128)(2,1)S(1)}, bf16[1024,512]{1,0:T(8,128)(2,1)S(1)}) custom-call(s32[6]{0:T(128)S(1)} %get-tuple-element.48.refs_0_, bf16[32,240,128]{2,1,0:T(8,128)(2,1)S(1)} %all_to_all.30.refs_1_, bf16[128,512]{1,0:T(8,128)(2,1)S(1)} %get-tuple-element.50.refs_2_, ...), custom_call_target="tpu_custom_call" | custom-call | flops 3000000000 | bytes 8000000 | tf_op jit(solution)/shard_map/cond/branch_1_fun/pallas_call | solution.py:130
  198.8 2.7 collective-permute-start.1
  201.5 2.3 collective-permute-done.1.refs_1_
  204.1 21.8 %all_to_all.31.refs_0_ = bf16[64,16,512]{2,1,0:T(8,128)(2,1)S(1)} all-to-all(bf16[64,16,512]{2,1,0:T(8,128)(2,1)S(1)} %bitcast.22), channel_id=1, replica_groups={{0,64,1,65,8,72,9,73,16,80,17,81,24,88,25,89,2,66,3,67,10,74,11,75,18,8..., dimensions={0} | all-to-all | bytes 2097152 | tf_op jit(solution)/shard_map/cond/branch_1_fun/all_to_all | solution.py:804
  226.1 29.0 %all_to_all.32 = bf16[64,16,512]{2,1,0:T(8,128)(2,1)S(1)} all-to-all(bf16[64,16,512]{2,1,0:T(8,128)(2,1)S(1)} %branch_1_fun.11), channel_id=1, replica_groups={{0,64,1,65,8,72,9,73,16,80,17,81,24,88,25,89,2,66,3,67,10,74,11,75,18,8..., dimensions={0} | all-to-all | bytes 2097152 | tf_op jit(solution)/shard_map/cond/branch_1_fun/all_to_all | solution.py:922
  256.0 1.9 collective-permute-start.2
  257.9 6.8 %shard_map.310 = (f32[512,2048]{1,0:T(8,128)}, f32[2048,512]{1,0:T(8,128)}, f32[512,1536]{1,0:T(8,128)}, f32[384,1024]{1,0:T(8,128)}, f32[512,512]{1,0:T(8,128)}...) custom-call(s32[6]{0:T(128)S(1)} %stack.27.refs_0_, ...), custom_call_target="tpu_custom_call" | custom-call | bytes 14000000 | tf_op jit(solution)/shard_map/pallas_call | solution.py:130
  264.9 3.9 %shard_map.311 = (f32[512,2048]{1,0:T(8,128)}, f32[2048,512]{1,0:T(8,128)}, f32[512,1536]{1,0:T(8,128)}, f32[384,1024]{1,0:T(8,128)}, f32[512,512]{1,0:T(8,128)}...) custom-call(s32[6]{0:T(128)S(1)} %stack.27.refs_0_, ...), custom_call_target="tpu_custom_call", output_to_operand_aliasing={{0}: (3, {}), {1}: (4, {}), {2}: (5, {}), {3}: (6, {}), {4}... | custom-call | bytes 14000000 | tf_op jit(solution)/shard_map/pallas_call | solution.py:130
  (45 shorter events, 5.9 us)
Async XLA Ops:
  7.8 16.1 %copy-start.12 = (bf16[512]{0:T(512)(128)(2,1)S(1)}, bf16[512]{0:T(512)(128)(2,1)}, u32[]{:S(2)}) copy-start(bf16[512]{0:T(512)(128)(2,1)} %param.32) | copy-start | bytes 3076
  7.8 16.7 %copy-start.13 = (bf16[512]{0:T(512)(128)(2,1)S(1)}, bf16[512]{0:T(512)(128)(2,1)}, u32[]{:S(2)}) copy-start(bf16[512]{0:T(512)(128)(2,1)} %param.33) | copy-start | bytes 3076
  7.8 17.3 %copy-start.14 = (bf16[512]{0:T(512)(128)(2,1)S(1)}, bf16[512]{0:T(512)(128)(2,1)}, u32[]{:S(2)}) copy-start(bf16[512]{0:T(512)(128)(2,1)} %param.37) | copy-start | bytes 3076
  7.9 17.9 %copy-start.15 = (bf16[512]{0:T(512)(128)(2,1)S(1)}, bf16[512]{0:T(512)(128)(2,1)}, u32[]{:S(2)}) copy-start(bf16[512]{0:T(512)(128)(2,1)} %param.38) | copy-start | bytes 3076
  12.7 39.5 %all-to-all-start.5 = ((bf16[32,240,128]{2,1,0:T(8,128)(2,1)}), bf16[32,240,128]{2,1,0:T(8,128)(2,1)S(1)}, u32[]{:S(2)}, u32[]{:S(2)}) async-start(bf16[32,240,128]{2,1,0:T(8,128)(2,1)} %get-tuple-element.124), calls=%async_computation.5 | async-start | bytes 3932160 | tf_op jit(solution)/shard_map/all_to_all | solution.py:767
  26.4 39.9 %copy-start.1 = (bf16[384,1024]{1,0:T(8,128)(2,1)S(1)}, bf16[384,1024]{1,0:T(8,128)(2,1)}, u32[]{:S(2)}) copy-start(bf16[384,1024]{1,0:T(8,128)(2,1)} %refs_18_.1) | copy-start | bytes 2359300
  61.0 14.1 %all-to-all-start.6 = ((bf16[32,16,128]{2,1,0:T(8,128)(2,1)}), bf16[32,16,128]{2,1,0:T(8,128)(2,1)S(1)}, u32[]{:S(2)}, u32[]{:S(2)}) async-start(bf16[32,16,128]{2,1,0:T(8,128)(2,1)} %get-tuple-element.125), calls=%async_computation.6 | async-start | bytes 262144 | tf_op jit(solution)/shard_map/all_to_all | solution.py:767
  66.0 9.8 %copy-start.9 = (bf16[1,128,512]{2,1,0:T(8,128)(2,1)S(1)}, bf16[1,128,512]{2,1,0:T(8,128)(2,1)}, u32[]{:S(2)}) copy-start(bf16[1,128,512]{2,1,0:T(8,128)(2,1)} %param.23) | copy-start | bytes 393220
  66.0 190.0 %all-gather.2.cloned.1.call-start = ((), (), s32[]{:S(2)}) async-start(), calls=%async_computation.7 | async-start | bytes 3194880 | tf_op jit(solution)/shard_map/all_gather | solution.py:907
  69.0 1.0 copy-start.2
  70.0 1.0 copy-start.3
  71.0 1.0 copy-start.4
  71.9 1.0 copy-start.5
  72.9 0.9 copy-start.6
  75.1 0.7 copy-start.10
  94.4 64.4 %copy-start.11 = (bf16[1,1024]{1,0:T(2,128)(2,1)S(1)}, bf16[1,1024]{1,0:T(2,128)(2,1)}, u32[]{:S(2)}) copy-start(bf16[1,1024]{1,0:T(2,128)(2,1)} %refs_4_.1) | copy-start | bytes 6148
  94.5 9.9 %collective-permute-start = (bf16[3072,512]{1,0:T(8,128)(2,1)}, bf16[3072,512]{1,0:T(8,128)(2,1)S(1)}, u32[]{:S(2)}, u32[]{:S(2)}) collective-permute-start(bf16[3072,512]{1,0:T(8,128)(2,1)} %get-tuple-element.42), channel_id=1, source_target_pairs={{0,32},{32,0},{64,96},{96,64},{1,33},{33,1},{65,97},{97,65},{8,40}... | collective-permute-start | bytes 9437192 | tf_op jit(solution)/shard_map/cond/branch_1_fun/ppermute | solution.py:771
  97.3 16.5 %all-to-all-start = ((bf16[32,16,128]{2,1,0:T(8,128)(2,1)}), bf16[32,16,128]{2,1,0:T(8,128)(2,1)S(1)}, u32[]{:S(2)}, u32[]{:S(2)}) async-start(bf16[32,16,128]{2,1,0:T(8,128)(2,1)} %get-tuple-element.40), calls=%async_computation | async-start | bytes 262144 | tf_op jit(solution)/shard_map/cond/branch_1_fun/all_to_all | solution.py:767
  107.0 1.7 copy-start
  113.8 43.8 %all-to-all-start.1 = ((bf16[64,48,512]{2,1,0:T(8,128)(2,1)}), bf16[64,48,512]{2,1,0:T(8,128)(2,1)S(1)}, u32[]{:S(2)}, u32[]{:S(2)}) async-start(bf16[64,48,512]{2,1,0:T(8,128)(2,1)} %bitcast.21), calls=%async_computation.1 | async-start | bytes 6291456 | tf_op jit(solution)/shard_map/cond/branch_1_fun/all_to_all | solution.py:804
  158.2 0.6 copy-start.8
  158.9 36.0 %copy-start.7 = (bf16[512,1536]{1,0:T(8,128)(2,1)S(1)}, bf16[512,1536]{1,0:T(8,128)(2,1)}, u32[]{:S(2)}) copy-start(bf16[512,1536]{1,0:T(8,128)(2,1)} %get-tuple-element.54.refs_6_) | copy-start | bytes 4718596 | tf_op jit(solution)/shard_map/cond
  158.9 36.0 %copy-start.16 = (bf16[384,512]{1,0:T(8,128)(2,1)S(1)}, bf16[384,512]{1,0:T(8,128)(2,1)}, u32[]{:S(2)}) copy-start(bf16[384,512]{1,0:T(8,128)(2,1)} %get-tuple-element.56.refs_8_) | copy-start | bytes 1179652 | tf_op jit(solution)/shard_map/cond
  158.9 36.0 %copy-start.17 = (f32[128,512]{1,0:T(8,128)S(1)}, f32[128,512]{1,0:T(8,128)}, u32[]{:S(2)}) copy-start(f32[128,512]{1,0:T(8,128)} %get-tuple-element.53.refs_5_) | copy-start | bytes 786436 | tf_op jit(solution)/shard_map/cond
  198.8 5.0 %collective-permute-start.1 = (bf16[1024,512]{1,0:T(8,128)(2,1)S(1)}, bf16[1024,512]{1,0:T(8,128)(2,1)S(1)}, u32[]{:S(2)}, u32[]{:S(2)}) collective-permute-start(bf16[1024,512]{1,0:T(8,128)(2,1)S(1)} %get-tuple-element.58), channel_id=1, source_target_pairs={{0,32},{32,0},{64,96},{96,64},{1,33},{33,1},{65,97},{97,65},{8,40}... | collective-permute-start | bytes 3145736 | tf_op jit(solution)/shard_map/cond/branch_1_fun/ppermute | solution.py:771
  256.0 8.9 %collective-permute-start.2 = (bf16[3072,512]{1,0:T(8,128)(2,1)}, bf16[3072,512]{1,0:T(8,128)(2,1)S(1)}, u32[]{:S(2)}, u32[]{:S(2)}) collective-permute-start(bf16[3072,512]{1,0:T(8,128)(2,1)} %all-gather.2.cloned.1.call-done.refs_1_), channel_id=1, source_target_pairs={{0,32},{32,0},{64,96},{96,64},{1,33},{33,1},{65,97},{97,65},{8,40}... | collective-permute-start | bytes 9437192 | tf_op jit(solution)/shard_map/ppermute | solution.py:771
  257.9 6.8 %collective-permute-start.3 = (bf16[1024,512]{1,0:T(8,128)(2,1)S(1)}, bf16[1024,512]{1,0:T(8,128)(2,1)S(1)}, u32[]{:S(2)}, u32[]{:S(2)}) collective-permute-start(bf16[1024,512]{1,0:T(8,128)(2,1)S(1)} %get-tuple-element.150.refs_2_), channel_id=1, source_target_pairs={{0,32},{32,0},{64,96},{96,64},{1,33},{33,1},{65,97},{97,65},{8,40}... | collective-permute-start | bytes 3145736 | tf_op jit(solution)/shard_map/ppermute | solution.py:771
Sparse Core Ops, SparseCore 0:
  158.9 96.9 all-gather.1
